TPU v7x, 128 devices: a whole 4x4x4 slice. The times are simulated.
128 devices in a mesh: grp: 2 (over core), dom: 64 (over y, z, x).
Axes of the slice: x: 4, y: 4, z: 4, core: 2. Of those that a mesh axis runs over, the one named last changes fastest.
Arguments:
- velocity: float32 [4096, 32, 256], P(('grp', 'dom')), may hold values from -6 to 6
- forcing: float32 [4096, 32, 256], P(('grp', 'dom')), may hold values from -3 to 3
- mass: float32 [4096, 32, 256], P(('grp', 'dom')), may hold values from 0.05 to 10
- sample_index: int32 [262144], P(('grp', 'dom')), may hold values from 0 to 262143
- partition: int32 [262144], P(('grp', 'dom')), may hold values from 0 to 262143, each once
- edge_source: int32 [1048576], P(('grp', 'dom')), may hold values from 0 to 2047
- edge_target: int32 [1048576], P(('grp', 'dom')), may hold values from 0 to 2047
- edge_valid: int32 [1048576], P(('grp', 'dom')), may hold values 0 or 1
- w_in: float32 [128], replicated, may hold values from -4 to 4
- b_in: float32 [128], replicated, may hold values from -3 to 3
- layer_weights: float32 [2, 256, 128], replicated, may hold values from -0.375 to 0.375
- layer_bias: float32 [2, 128], replicated, may hold values from -2 to 2
- w_out: float32 [128], replicated, may hold values from -0.5 to 0.5
Outputs:
- new_velocity: float32 [4096, 32, 256], P(('grp', 'dom'))
- loss: float32 [], replicated
- grad_w_in: float32 [128], replicated
- grad_b_in: float32 [128], replicated
- grad_layer_weights: float32 [2, 256, 128], replicated
- grad_layer_bias: float32 [2, 128], replicated
- grad_w_out: float32 [128], replicated
Inputs may be any that keep to these rules, and one draw needn't show every extreme that they name: partition names every sampled node exactly once.
All inputs are finite; a program needn't handle non-finite values. No bound on the sum of `edge_valid` on one device may be relied on, other than what follows from the above.
Results may differ from a plain program's by a relative error of at most 0.0006.
Values sent between devices are 32-bit elements; how exact they have to be, the bound alone decides.
A program may use at most 128 MiB of HBM per device.

v0:
```python
import jax
import jax.numpy as jnp
from jax import lax
from jax.sharding import PartitionSpec as P

STEPS = 2
ITERS = 6
LAYERS = 2


penalty = 2.0
agg_scale = 0.25


def with_halo(block, sides, width):
    for axis, dim in sides:
        count = lax.axis_size(axis)
        forward = [(i, i + 1) for i in range(count - 1)]
        forward.append((count - 1, 0))
        backward = [(target, source) for source, target in forward]
        low = lax.ppermute(
            lax.slice_in_dim(block, block.shape[dim] - width, None, axis=dim), axis, forward
        )
        high = lax.ppermute(lax.slice_in_dim(block, 0, width, axis=dim), axis, backward)
        block = jnp.concatenate([low, block, high], axis=dim)
    return block


def block_stiffness(length):
    rows = jnp.arange(length, dtype=jnp.int32)[:, None]
    cols = jnp.arange(length, dtype=jnp.int32)[None, :]
    spread = jnp.abs(rows % 8 - cols % 8).astype(jnp.float32)
    local = 2.5 * (rows % 8 == cols % 8).astype(jnp.float32) - jnp.exp(-spread)
    return jnp.where(rows // 8 == cols // 8, local, 0.0)


def operate(field, mass, matrices):
    stream_mat, normal_mat, span_mat = matrices
    padded = with_halo(field, ((("grp", "dom"), 0),), 1)
    total = jnp.einsum("ij,jyz->iyz", stream_mat, field, precision=lax.Precision.HIGHEST)
    total = total + jnp.einsum("ij,xjz->xiz", normal_mat, field, precision=lax.Precision.HIGHEST)
    total = total + jnp.einsum("xyj,jk->xyk", field, span_mat, precision=lax.Precision.HIGHEST)
    stream_len, normal_len, span_len = field.shape
    place_x = jnp.arange(stream_len, dtype=jnp.int32)[:, None, None]
    jumps = jnp.where(place_x % 8 == 7, field - padded[2:], 0.0) + jnp.where(
        place_x % 8 == 0, field - padded[:-2], 0.0
    )
    place_y = jnp.arange(normal_len, dtype=jnp.int32)[None, :, None]
    following = jnp.roll(field, -1, 1)
    preceding = jnp.roll(field, 1, 1)
    jumps = jumps + jnp.where(
        (place_y % 8 == 7) & (place_y < normal_len - 1), field - following, 0.0
    )
    jumps = jumps + jnp.where((place_y % 8 == 0) & (place_y > 0), field - preceding, 0.0)
    place_z = jnp.arange(span_len, dtype=jnp.int32)[None, None, :]
    jumps = jumps + jnp.where(place_z % 8 == 7, field - jnp.roll(field, -1, 2), 0.0)
    jumps = jumps + jnp.where(place_z % 8 == 0, field - jnp.roll(field, 1, 2), 0.0)
    return mass * field + total + penalty * jumps


def squares(residual):
    return lax.psum(jnp.sum(residual * residual), ("grp", "dom"))


def encode(w_in, b_in, feats):
    return jnp.tanh(feats[:, None] * w_in[None, :] + b_in[None, :])


def propagate(weight, bias, state, source, target_node, valid):
    carried = state[source] * valid[:, None].astype(jnp.float32)
    summed = jax.ops.segment_sum(carried, target_node, num_segments=state.shape[0]) * agg_scale
    joined = jnp.concatenate([state, summed], axis=1)
    return state + jnp.tanh(
        jnp.dot(joined, weight, precision=lax.Precision.HIGHEST) + bias[None, :]
    )


def readout(w_out, state, target, total):
    pred = jnp.dot(state, w_out, precision=lax.Precision.HIGHEST)
    return jnp.sum((pred - target) ** 2) / total


def shards(
    velocity,
    forcing,
    mass,
    sample_index,
    partition,
    edge_source,
    edge_target,
    edge_valid,
    w_in,
    b_in,
    layer_weights,
    layer_bias,
    w_out,
):
    matrices = (
        block_stiffness(velocity.shape[0]),
        block_stiffness(velocity.shape[1]),
        block_stiffness(velocity.shape[2]),
    )
    field = velocity
    samples = []
    for step in range(STEPS):
        rhs = mass * field + forcing
        guess = field
        residual = rhs - operate(guess, mass, matrices)
        direction = residual
        norm_now = squares(residual)
        for it in range(ITERS):
            image = operate(direction, mass, matrices)
            alpha = norm_now / lax.psum(jnp.sum(direction * image), ("grp", "dom"))
            guess = guess + alpha * direction
            residual = residual - alpha * image
            norm_next = squares(residual)
            direction = residual + norm_next / norm_now * direction
            norm_now = norm_next
        field = guess
        samples.append(field.reshape(-1)[sample_index])
    whole = lax.all_gather(jnp.stack(samples), ("grp", "dom"), axis=1, tiled=True)
    first_row, last_row = (whole[0], whole[STEPS - 1])
    feats = first_row[partition]
    target = last_row[partition]
    total_nodes = jnp.float32(feats.shape[0] * lax.axis_size("grp") * lax.axis_size("dom"))
    states = [encode(w_in, b_in, feats)]
    for layer in range(LAYERS):
        states.append(
            propagate(
                layer_weights[layer],
                layer_bias[layer],
                states[-1],
                edge_source,
                edge_target,
                edge_valid,
            )
        )
    local_loss, head_pull = jax.vjp(
        lambda weight, state: readout(weight, state, target, total_nodes), w_out, states[-1]
    )
    grad_out, grad_state = head_pull(jnp.float32(1.0))
    weight_grads = [None] * LAYERS
    bias_grads = [None] * LAYERS
    for layer in reversed(range(LAYERS)):
        dummy, layer_pull = jax.vjp(
            lambda weight, bias, state: propagate(
                weight, bias, state, edge_source, edge_target, edge_valid
            ),
            layer_weights[layer],
            layer_bias[layer],
            states[layer],
        )
        grad_weight, grad_bias, grad_state = layer_pull(grad_state)
        weight_grads[layer] = grad_weight
        bias_grads[layer] = grad_bias
    dummy, input_pull = jax.vjp(lambda weight, bias: encode(weight, bias, feats), w_in, b_in)
    grad_win, grad_bin = input_pull(grad_state)
    stacked_weights = jnp.stack(weight_grads)
    stacked_bias = jnp.stack(bias_grads)
    local_loss, grad_win, grad_bin, stacked_weights, stacked_bias, grad_out = lax.psum(
        (local_loss, grad_win, grad_bin, stacked_weights, stacked_bias, grad_out), ("grp", "dom")
    )
    return (field, local_loss, grad_win, grad_bin, stacked_weights, stacked_bias, grad_out)


def solution(mesh):
    return jax.shard_map(
        shards,
        mesh=mesh,
        in_specs=(
            P(("grp", "dom"), None, None),
            P(("grp", "dom"), None, None),
            P(("grp", "dom"), None, None),
            P(("grp", "dom")),
            P(("grp", "dom")),
            P(("grp", "dom")),
            P(("grp", "dom")),
            P(("grp", "dom")),
            P(),
            P(),
            P(),
            P(),
            P(),
        ),
        out_specs=(P(("grp", "dom"), None, None), P(), P(), P(), P(), P(), P()),
        check_vma=False,
    )
```

profile of v0, /device:TPU:1, one launch (start us, length us, event | category | flops | bytes accessed | tf_op | source)
XLA Modules:
  0.0 2283.4 jit_solution(14933641382648994517)
XLA Ops:
  115.5 63.4 %psum.212 = f32[]{:T(128)} all-reduce(f32[]{:T(128)} %multiply_reduce_fusion.20), channel_id=1, replica_groups=mesh['grp'=2,'dom'=64] {'grp','dom'}, use_global_device_ids=true, to_apply=%region_5.6 | all-reduce | flops 1 | bytes 8 | tf_op jit(solution)/shard_map/psum | solution.py:62
  200.4 62.0 %psum.213 = f32[]{:T(128)} all-reduce(f32[]{:T(128)} %get-tuple-element.203), channel_id=1, replica_groups=mesh['grp'=2,'dom'=64] {'grp','dom'}, use_global_device_ids=true, to_apply=%region_7.8 | all-reduce | flops 1 | bytes 8 | tf_op jit(solution)/shard_map/psum | solution.py:113
  266.7 63.6 %psum.214 = f32[]{:T(128)} all-reduce(f32[]{:T(128)} %get-tuple-element.46), channel_id=1, replica_groups=mesh['grp'=2,'dom'=64] {'grp','dom'}, use_global_device_ids=true, to_apply=%region_9.10 | all-reduce | flops 1 | bytes 8 | tf_op jit(solution)/shard_map/psum | solution.py:62
  352.6 62.0 %psum.215 = f32[]{:T(128)} all-reduce(f32[]{:T(128)} %get-tuple-element.205), channel_id=1, replica_groups=mesh['grp'=2,'dom'=64] {'grp','dom'}, use_global_device_ids=true, to_apply=%region_11.12 | all-reduce | flops 1 | bytes 8 | tf_op jit(solution)/shard_map/psum | solution.py:113
  419.0 63.6 %psum.216 = f32[]{:T(128)} all-reduce(f32[]{:T(128)} %get-tuple-element.44), channel_id=1, replica_groups=mesh['grp'=2,'dom'=64] {'grp','dom'}, use_global_device_ids=true, to_apply=%region_13.14 | all-reduce | flops 1 | bytes 8 | tf_op jit(solution)/shard_map/psum | solution.py:62
  571.2 63.6 %psum.218 = f32[]{:T(128)} all-reduce(f32[]{:T(128)} %get-tuple-element.42), channel_id=1, replica_groups=mesh['grp'=2,'dom'=64] {'grp','dom'}, use_global_device_ids=true, to_apply=%region_17.18 | all-reduce | flops 1 | bytes 8 | tf_op jit(solution)/shard_map/psum | solution.py:62
  722.7 63.6 %psum.220 = f32[]{:T(128)} all-reduce(f32[]{:T(128)} %multiply_reduce_fusion.12), channel_id=1, replica_groups=mesh['grp'=2,'dom'=64] {'grp','dom'}, use_global_device_ids=true, to_apply=%region_21.22 | all-reduce | flops 1 | bytes 8 | tf_op jit(solution)/shard_map/psum | solution.py:62
  807.9 62.0 %psum.221 = f32[]{:T(128)} all-reduce(f32[]{:T(128)} %fusion.290), channel_id=1, replica_groups=mesh['grp'=2,'dom'=64] {'grp','dom'}, use_global_device_ids=true, to_apply=%region_23.24 | all-reduce | flops 1 | bytes 8 | tf_op jit(solution)/shard_map/psum | solution.py:113
  910.7 62.2 %all-reduce.1 = (f32[]{:T(128)}, f32[]{:T(128)}) all-reduce(f32[]{:T(128)} %get-tuple-element.24, f32[]{:T(128)} %get-tuple-element.23), channel_id=1, replica_groups=mesh['grp'=2,'dom'=64] {'grp','dom'}, use_global_device_ids=true, to_apply=%region_25.26 | all-reduce | flops 2 | bytes 16 | tf_op jit(solution)/shard_map/psum | solution.py:62
  976.7 63.8 %psum.224 = f32[]{:T(128)} all-reduce(f32[]{:T(128)} %multiply_reduce_fusion.9), channel_id=1, replica_groups=mesh['grp'=2,'dom'=64] {'grp','dom'}, use_global_device_ids=true, to_apply=%region_29.30 | all-reduce | flops 1 | bytes 8 | tf_op jit(solution)/shard_map/psum | solution.py:62
  1063.1 62.4 %psum.225 = f32[]{:T(128)} all-reduce(f32[]{:T(128)} %get-tuple-element.212), channel_id=1, replica_groups=mesh['grp'=2,'dom'=64] {'grp','dom'}, use_global_device_ids=true, to_apply=%region_31.32 | all-reduce | flops 1 | bytes 8 | tf_op jit(solution)/shard_map/psum | solution.py:113
  1130.2 63.2 %psum.226 = f32[]{:T(128)} all-reduce(f32[]{:T(128)} %get-tuple-element.40), channel_id=1, replica_groups=mesh['grp'=2,'dom'=64] {'grp','dom'}, use_global_device_ids=true, to_apply=%region_33.34 | all-reduce | flops 1 | bytes 8 | tf_op jit(solution)/shard_map/psum | solution.py:62
  1215.9 62.2 %psum.227 = f32[]{:T(128)} all-reduce(f32[]{:T(128)} %get-tuple-element.214), channel_id=1, replica_groups=mesh['grp'=2,'dom'=64] {'grp','dom'}, use_global_device_ids=true, to_apply=%region_35.36 | all-reduce | flops 1 | bytes 8 | tf_op jit(solution)/shard_map/psum | solution.py:113
  1282.8 63.4 %psum.228 = f32[]{:T(128)} all-reduce(f32[]{:T(128)} %get-tuple-element.38), channel_id=1, replica_groups=mesh['grp'=2,'dom'=64] {'grp','dom'}, use_global_device_ids=true, to_apply=%region_37.38 | all-reduce | flops 1 | bytes 8 | tf_op jit(solution)/shard_map/psum | solution.py:62
  1368.7 62.2 %psum.229 = f32[]{:T(128)} all-reduce(f32[]{:T(128)} %get-tuple-element.216), channel_id=1, replica_groups=mesh['grp'=2,'dom'=64] {'grp','dom'}, use_global_device_ids=true, to_apply=%region_39.40 | all-reduce | flops 1 | bytes 8 | tf_op jit(solution)/shard_map/psum | solution.py:113
  1435.3 63.6 %psum.230 = f32[]{:T(128)} all-reduce(f32[]{:T(128)} %get-tuple-element.36), channel_id=1, replica_groups=mesh['grp'=2,'dom'=64] {'grp','dom'}, use_global_device_ids=true, to_apply=%region_41.42 | all-reduce | flops 1 | bytes 8 | tf_op jit(solution)/shard_map/psum | solution.py:62
  1521.7 62.2 %psum.231 = f32[]{:T(128)} all-reduce(f32[]{:T(128)} %get-tuple-element.218), channel_id=1, replica_groups=mesh['grp'=2,'dom'=64] {'grp','dom'}, use_global_device_ids=true, to_apply=%region_43.44 | all-reduce | flops 1 | bytes 8 | tf_op jit(solution)/shard_map/psum | solution.py:113
  1589.3 63.3 %psum.232 = f32[]{:T(128)} all-reduce(f32[]{:T(128)} %multiply_reduce_fusion.1), channel_id=1, replica_groups=mesh['grp'=2,'dom'=64] {'grp','dom'}, use_global_device_ids=true, to_apply=%region_45.46 | all-reduce | flops 1 | bytes 8 | tf_op jit(solution)/shard_map/psum | solution.py:62
  1699.1 62.7 %psum.233 = f32[]{:T(128)} all-reduce(f32[]{:T(128)} %fusion.291), channel_id=1, replica_groups=mesh['grp'=2,'dom'=64] {'grp','dom'}, use_global_device_ids=true, to_apply=%region_47.48 | all-reduce | flops 1 | bytes 8 | tf_op jit(solution)/shard_map/psum | solution.py:113
  1859.5 70.1 %scatter_custom_fusion = f32[2048,128]{1,0:T(8,128)S(1)} fusion(s32[8192]{0:T(1024)S(1)} %copy-done.24, f32[8192]{0:T(1024)S(1)} %convert_element_type.99, f32[]{:T(128)} %constant.419.clone.1, f32[2048,128]{1,0:T(8,128)S(1)} %add_tanh_fusion, s32[8192]{0:T(1024)S(1)} %get-tuple-element.196), kind=kCustom, calls=%fused_computation.20 | custom fusion | flops 2097152 | bytes 2162692 | tf_op jit(solution)/shard_map/scatter-add | solution.py:71
  1933.1 70.7 %scatter_custom_fusion.1 = f32[2048,128]{1,0:T(8,128)} fusion(s32[8192]{0:T(1024)S(1)} %copy-done.24, f32[8192]{0:T(1024)S(1)} %convert_element_type.99, f32[]{:T(128)} %constant.419.clone.1, f32[2048,128]{1,0:T(8,128)S(1)} %get-tuple-element.220, s32[8192]{0:T(1024)S(1)} %get-tuple-element.196), kind=kCustom, calls=%fused_computation.18 | custom fusion | flops 2097152 | bytes 2162692 | tf_op jit(solution)/shard_map/scatter-add | solution.py:71
  2030.3 96.9 %scatter_custom_fusion.2 = f32[2048,128]{1,0:T(8,128)S(1)} fusion(f32[2048,128]{1,0:T(8,128)S(1)} %get-tuple-element.51, s32[8192]{0:T(1024)} %get-tuple-element.195, f32[]{:T(128)} %constant.419.clone.1, f32[8192]{0:T(1024)S(1)} %convert_element_type.99, pred[8192]{0:T(1024)(128)(4,1)S(1)} %compare_and_fusion, f32[2048,128]{1,0:T(8,128)} %get-tuple-element.50, ...), kind=kCustom, calls=%fused_computation.15 | custom fusion | flops 3145728 | bytes 2171392 | tf_op jit(solution)/shard_map/transpose(jvp())/scatter-add | solution.py:70
  2138.5 69.8 %scatter_custom_fusion.3 = f32[2048,128]{1,0:T(8,128)} fusion(f32[2048,128]{1,0:T(8,128)} %get-tuple-element.49, s32[8192]{0:T(1024)} %get-tuple-element.195, f32[]{:T(128)} %constant.419.clone.1, f32[8192]{0:T(1024)S(1)} %convert_element_type.99, pred[8192]{0:T(1024)(128)(4,1)S(1)} %compare_and_fusion, f32[2048,128]{1,0:T(8,128)S(1)} %get-tuple-element.48, ...), kind=kCustom, calls=%fused_computation.12 | custom fusion | flops 3145728 | bytes 2171392 | tf_op jit(solution)/shard_map/transpose(jvp())/scatter-add | solution.py:70
  2211.3 62.7 %all-reduce = (f32[]{:T(128)}, f32[128]{0:T(128)}, f32[128]{0:T(128)}, f32[2,128]{1,0:T(2,128)}, f32[128]{0:T(128)}) all-reduce(f32[]{:T(128)S(6)} %div.203, f32[128]{0:T(128)S(1)} %get-tuple-element.22, f32[128]{0:T(128)S(1)} %get-tuple-element.21, ...), channel_id=1, replica_groups=mesh['grp'=2,'dom'=64] {'grp','dom'}, use_global_device_ids=true, to_apply=%region_51.52 | all-reduce | flops 641 | bytes 5128 | tf_op jit(solution)/shard_map/psum | solution.py:160
  (351 shorter events, 672.3 us)
Async XLA Ops:
  7.2 1836.1 %all-gather.2.cloned.1.call-start = ((), (), s32[]{:S(2)}) async-start(), calls=%async_computation | async-start | bytes 2113536 | tf_op jit(solution)/shard_map/all_gather | solution.py:121
  8.0 16.4 collective-permute-start
  17.9 8.8 collective-permute-start.1
  34.0 6.1 collective-permute-start.2
  38.9 9.0 collective-permute-start.3
  184.3 3.5 collective-permute-start.4
  186.8 9.2 collective-permute-start.5
  339.2 8.9 collective-permute-start.7
  491.4 9.0 collective-permute-start.9
  643.7 9.2 collective-permute-start.11
  795.4 8.9 collective-permute-start.13
  878.6 4.5 collective-permute-start.14
  882.1 9.0 collective-permute-start.15
  898.4 8.8 collective-permute-start.17
  1049.2 9.4 collective-permute-start.19
  1199.9 3.7 collective-permute-start.20
  1202.6 8.8 collective-permute-start.21
  1352.8 3.8 collective-permute-start.22
  1355.5 8.8 collective-permute-start.23
  1505.7 3.8 collective-permute-start.24
  1508.5 8.8 collective-permute-start.25
  1659.6 3.8 collective-permute-start.26
  1662.4 8.8 collective-permute-start.27
  1780.8 493.7 %all-reduce.5.cloned.1.call-start = ((), (), s32[]{:S(2)}) async-start(), calls=%async_computation.1 | async-start | bytes 524288 | tf_op jit(solution)/shard_map/psum | solution.py:160
  (61 other events, 1899.9 us)
Sparse Core Ops, SparseCore 0:
  1780.9 62.3 all-gather.1
  2135.9 138.5 all-reduce.4
where the time goes:
time: 2300 us; the launch traced here: 2280 us
  blocking collectives  1440 us (63%)
  other arithmetic  364 us (16%)
  waiting for transfers between devices  177 us (8%)
  matrix products  118 us (5%)
  local copies, waits for them, and re-layouts  88.1 us (4%)
  starting transfers between devices  46.5 us (2%)
  between operations  46.1 us (2%)
    psum x12, blocking collectives, squares(): return lax.psum(jnp.sum(residual * residual), ('grp', 'dom'))  759 us
    psum x10, blocking collectives, shards(): alpha = norm_now / lax.psum(jnp.sum(direction * image), ('grp', 'dom'))  621 us
    scatter-add x2, other arithmetic, propagate(): carried = state[source] * valid[:, None].astype(jnp.float32)  167 us
    scatter-add x2, other arithmetic, propagate(): jax.ops.segment_sum(carried, target_node, num_segments=state.shape[0])  141 us
    ppermute x14, waiting for transfers between devices, with_halo(): lax.ppermute(lax.slice_in_dim(block, block.shape[dim] - width, None, axis...  103 us
    psum x1, blocking collectives, shards(): lax.psum((local_loss, grad_win, grad_bin, stacked_weights, stacked_bias,...  62.7 us
    all_gather x1, waiting for transfers between devices, shards(): lax.all_gather(jnp.stack(samples), ('grp', 'dom'), axis=1, tiled=True)  61.2 us
    dot_general x14, matrix products, operate(): jnp.einsum('ij,jyz->iyz', stream_mat, field, precision=lax.Precision.HIGH...  56.6 us
  transfers between devices with their start and end apart: 30, of which 29 were waited for; matrix products, arithmetic and copies ran while one was open for 4% of the time, Pallas kernels for 0%

commit v1 on v0

v1 whole, which is shorter than its diff:
```python
import functools

import jax
import jax.numpy as jnp
import ml_dtypes
import numpy as np
from jax import lax
from jax.experimental import pallas as pl
from jax.experimental.pallas import tpu as pltpu
from jax.sharding import PartitionSpec as P

MESH = pl.DeviceIdType.MESH
F32 = jnp.float32
BF16 = jnp.bfloat16

STEPS = 2
LAYERS = 2
PENALTY = 2.0
AGG_SCALE = 0.25
NODES = 2048
EDGES = 8192
ROWS = 1024
PLANE = 32
GROUPS, DOMS, LINE, SHEET = 2, 64, 4, 16

CENTER = 14.125
HALF = 12.575
GAIN = 2.0 / HALF
PIVOT = 1e-6
REACH = GAIN * GAIN * float(sum(np.exp(-2.0 * i) for i in range(1, 8)))
CHIP_ORDER = [0] + sorted(
    range(1, DOMS), key=lambda o: -sum(min(c, 4 - c) for c in (o % 4, o // 4 % 4, o // 16))
)
FAR_ORDER = [0] + sorted(range(1, 16), key=lambda o: -(min(o % 4, 4 - o % 4) + min(o // 4, 4 - o // 4)))


def split_np(matrix):
    high = matrix.astype(np.float32).astype(ml_dtypes.bfloat16)
    low = (matrix - high.astype(np.float64)).astype(np.float32).astype(ml_dtypes.bfloat16)
    return high, low


def element_matrix():
    at = np.arange(8)
    return 2.5 * np.eye(8) - np.exp(-np.abs(at[:, None] - at[None, :]).astype(np.float64))


def line_matrix(length, wrap):
    matrix = np.kron(np.eye(length // 8), element_matrix())
    for last in range(7, length, 8):
        follow = (last + 1) % length
        if follow == 0 and not wrap:
            continue
        matrix[last, last] += PENALTY
        matrix[follow, follow] += PENALTY
        matrix[last, follow] -= PENALTY
        matrix[follow, last] -= PENALTY
    return matrix


def field_matrices():
    ends = np.zeros(8)
    ends[0] = ends[7] = PENALTY
    sheet = np.kron(element_matrix() + np.diag(ends), np.eye(32)) + np.kron(np.eye(8), line_matrix(32, False))
    sheet_high, sheet_low = split_np(GAIN * sheet)
    span_high, span_low = split_np(GAIN * line_matrix(256, True))
    left = np.concatenate([sheet_high, sheet_low, sheet_high], axis=1)
    right = np.concatenate([span_high, span_low, span_high], axis=0)
    edge = np.concatenate([sheet_high[:32, :32], sheet_low[:32, :32], sheet_high[:32, :32]], axis=1)
    return left, right, edge


def split(value):
    high = value.astype(BF16)
    return high, (value - high.astype(F32)).astype(BF16)


def mm(left, right):
    return jnp.dot(left, right, preferred_element_type=F32)


def mm_lanes(left, right):
    return lax.dot_general(left, right, (((1,), (1,)), ((), ())), preferred_element_type=F32)


def wide(tile):
    two = jnp.concatenate([tile, tile], axis=1)
    return jnp.concatenate([two, two], axis=0)


def fold(value):
    half = value[:8] + value[8:]
    return half[:, :128] + half[:, 128:]


def solve(matrix, rhs):
    n = len(rhs)
    rows = [list(row) for row in matrix]
    right = list(rhs)
    lower = {}
    inverse = []
    for k in range(n):
        pivot = rows[k][k]
        inverse.append(jnp.where(pivot > PIVOT * matrix[k][k], 1.0 / pivot, 0.0))
        for i in range(k + 1, n):
            factor = rows[k][i] * inverse[k]
            lower[i, k] = factor
            for j in range(i, n):
                rows[i][j] = rows[i][j] - factor * rows[k][j]
            right[i] = right[i] - factor * right[k]
    out = [None] * n
    for k in reversed(range(n)):
        value = right[k] * inverse[k]
        for i in range(k + 1, n):
            value = value - lower[i, k] * out[i]
        out[k] = value
    return out


def image_rows(gram, count):
    out = []
    for i in range(count):
        out.append(
            [CENTER * a + (0.5 * HALF) * (b + c) for a, b, c in zip(gram[i], gram[i + 1], gram[abs(i - 1)])]
        )
    return out


def image_coefs(coefs):
    out = [None] * (len(coefs) + 1)

    def add(at, value):
        out[at] = value if out[at] is None else out[at] + value

    for j, c in enumerate(coefs):
        add(j, CENTER * c)
        if j == 0:
            add(1, HALF * c)
        else:
            add(j + 1, (0.5 * HALF) * c)
            add(j - 1, (0.5 * HALF) * c)
    return out


def index_row(index_ref, i):
    return jnp.concatenate([index_ref[2 * i : 2 * i + 1, :], index_ref[2 * i + 1 : 2 * i + 2, :]], axis=1)


def onehot_rows(index_ref, out_ref):
    for i in range(8):
        row = index_row(index_ref, i) >> 8

        def body(c, carry):
            at = pl.multiple_of(c * 128, 128)
            place = lax.broadcasted_iota(jnp.int32, (128, 256), 0) + at
            out_ref[pl.ds(at, 128), i * 256 : (i + 1) * 256] = jnp.where(place == row, 1.0, 0.0).astype(BF16)
            return carry

        lax.fori_loop(0, ROWS // 128, body, 0)


def pick(table, index_ref, onehot_ref, write):
    both = jnp.concatenate(split(table.T), axis=0)
    place = lax.broadcasted_iota(jnp.int32, (256, 256), 0)
    for i in range(8):
        rows = mm(both, onehot_ref[:, i * 256 : (i + 1) * 256])
        rows = rows[:256] + rows[256:]
        column = index_row(index_ref, i) & 255
        write(i, jnp.sum(jnp.where(place == column, rows, 0.0), axis=0, keepdims=True))


def shifted(coefs):
    out = [None] * (len(coefs) + 1)

    def add(at, value):
        out[at] = value if out[at] is None else out[at] + value

    for i, c in enumerate(coefs):
        if i == 0:
            add(1, c)
        else:
            add(i + 1, 0.5 * c)
            add(i - 1, 0.5 * c)
    return out


def merged(parts):
    out = []
    for factor, coefs in parts:
        for i, c in enumerate(coefs):
            value = c if factor is None else factor * c
            if i < len(out):
                out[i] = out[i] + value
            else:
                out.append(value)
    return out


def core_peer(grp, dom, o):
    hop = CHIP_ORDER[o]
    y, z, x = (dom // 16 + hop // 16) % 4, (dom // 4 + hop // 4) % 4, (dom + hop) % 4
    return grp, y * 16 + z * 4 + x


def steps_kernel(
    vel, force, mass, sample, part, left_mat, right_mat, edge_mat,
    out, feats, target,
    basis, stage, ghost, first, beside, dots, near, far, table, hot_sample, hot_part,
    halo_s, halo_r, first_s, first_r, near_s, near_r, far_s, far_r, peer_s, peer_r, core_s, core_r,
):
    grp = lax.axis_index("grp")
    dom = lax.axis_index("dom")
    me = grp * DOMS + dom
    line = dom % LINE
    sheet = dom // LINE
    near_me = grp * LINE + line

    def near_peer(o):
        other = (near_me + o) % (GROUPS * LINE)
        return other, (other // LINE, sheet * LINE + other % LINE)

    def far_peer(o):
        hop = FAR_ORDER[o]
        other = (sheet // 4 + hop // 4) % 4 * 4 + (sheet + hop) % 4
        return other, (grp, other * LINE + line)

    other_core = (1 - grp, dom)
    after = (me + 1) % (GROUPS * DOMS)
    before = (me + GROUPS * DOMS - 1) % (GROUPS * DOMS)
    after_id = (after // DOMS, after % DOMS)
    before_id = (before // DOMS, before % DOMS)

    barrier = pltpu.get_barrier_semaphore()
    greeted = [core_peer(grp, dom, o) for o in range(1, DOMS)] + [near_peer(o)[1] for o in range(1, 8)]
    greeted += [after_id, before_id]
    for who in greeted:
        pl.semaphore_signal(barrier, inc=1, device_id=who, device_id_type=MESH)
    pl.semaphore_wait(barrier, len(greeted))

    def remote(src, dst, send, recv, who):
        return pltpu.make_async_remote_copy(
            src_ref=src, dst_ref=dst, send_sem=send, recv_sem=recv, device_id=who, device_id_type=MESH
        )

    sides = ((0, 0, 0, before_id), (1, ROWS - PLANE, 7, after_id))
    pull = PENALTY * GAIN

    def products(source, e):
        high, low = split(source[e * 256 : (e + 1) * 256, :])
        rows = mm(left_mat[...], jnp.concatenate([high, high, low], axis=0))
        return rows + mm(jnp.concatenate([high, high, low], axis=1), right_mat[...])

    def store_inner(dest, source, e, value, scale):
        at = e * 256
        top, bottom = value[:PLANE], value[256 - PLANE :]
        if e > 0:
            top = top - scale * source[at - PLANE : at, :]
        if e < 3:
            bottom = bottom - scale * source[at + 256 : at + 256 + PLANE, :]
        dest[at : at + PLANE, :] = top
        dest[at + PLANE : at + 256 - PLANE, :] = value[PLANE : 256 - PLANE]
        dest[at + 256 - PLANE : at + 256, :] = bottom

    def expand(slot, opening, elements):
        src, dst = basis.at[slot], basis.at[slot + 1]
        for e in elements:
            rows = pl.ds(e * 256, 256)
            value = products(src, e) + (GAIN * mass[rows, :] - GAIN * CENTER) * src[rows, :]
            if opening:
                value = 0.5 * value
            else:
                value = value - basis[slot - 1, rows, :]
            store_inner(dst, src, e, value, pull * (0.5 if opening else 1.0))

    def outer(slot, side, plane, scale):
        at = sides[side][1]
        value = basis[slot, at : at + PLANE, :] - scale * plane
        basis[slot, at : at + PLANE, :] = value
        return value

    def along(plane, level, near_rows):
        high, low = split(plane)
        wide_plane = jnp.concatenate([high, high, low], axis=1)
        return near_rows + mm(wide_plane, right_mat[...]) + (GAIN * level - GAIN * CENTER) * plane

    def edge_map(side, plane):
        high, low = split(plane)
        rows = mm(edge_mat[...], jnp.concatenate([high, high, low], axis=0))
        return along(plane, first[side, 1], rows)

    def exchange_copies(ex):
        return [
            remote(stage.at[ex, side], ghost.at[ex, 1 - side], halo_s.at[ex, side], halo_r.at[ex, 1 - side], who)
            for side, _, _, who in sides
        ]

    def exchange_send(ex, slot):
        for side, at, place, _ in sides:
            e = 0 if side == 0 else 3
            high, low = split(basis[slot + 1, e * 256 : (e + 1) * 256, :])
            rows = mm(left_mat[place * PLANE : (place + 1) * PLANE, :], jnp.concatenate([high, high, low], axis=0))
            plane = basis[slot + 1, at : at + PLANE, :]
            own = basis[slot, at : at + PLANE, :]
            stage[ex, side, 0] = own
            stage[ex, side, 1] = plane
            stage[ex, side, 2] = along(plane, mass[at : at + PLANE, :], rows) - own
        for copy in exchange_copies(ex):
            copy.start()

    def exchange_wait(ex, slot, opening):
        for copy in exchange_copies(ex):
            copy.wait()
        scale = pull * (0.5 if opening else 1.0)
        for side, at, _, _ in sides:
            own = basis[slot, at : at + PLANE, :]
            then = outer(slot + 1, side, ghost[ex, side, 0], scale)
            beside[side, 0] = ghost[ex, side, 1] - scale * own
            beside[side, 1] = ghost[ex, side, 2] - scale * edge_map(side, own) - pull * then

    def follow(slot):
        for k in range(2):
            expand(slot + k, False, range(4))
            for side in range(2):
                outer(slot + k + 1, side, beside[side, k], pull)

    def accumulate(pairs, chunks):
        slots = sorted({a for _, a, _ in pairs} | {b for _, _, b in pairs})

        def body(c, carry):
            at = pl.multiple_of(c * 16, 16)
            rows = {s: basis[s, pl.ds(at, 16), :] for s in slots}
            return tuple(acc + fold(rows[a] * rows[b]) for acc, (_, a, b) in zip(carry, pairs))

        carry = tuple(jnp.zeros((8, 128), F32) for _ in pairs)
        carry = lax.fori_loop(0, chunks, body, carry, unroll=4)
        for (i, _, _), acc in zip(pairs, carry):
            dots[i] = acc

    stages = (
        (near, near_s, near_r, near_peer, near_me, GROUPS * LINE),
        (far, far_s, far_r, far_peer, sheet, SHEET),
    )

    def reduce_send(call, which, message):
        buffer, send, recv, peer, mine, n = stages[which]
        buffer[call, mine] = jnp.broadcast_to(message, (8, 128))
        own = buffer.at[call, mine]
        for o in range(1, n):
            remote(own, own, send.at[call, o], recv.at[call, mine], peer(o)[1]).start()

    def reduce_wait(call, which):
        buffer, send, recv, peer, mine, n = stages[which]
        own = buffer.at[call, mine]
        for o in range(1, n):
            other, who = peer(o)
            slot = buffer.at[call, other]
            remote(slot, slot, send.at[call, o], recv.at[call, other], who).wait_recv()
        for o in range(1, n):
            remote(own, own, send.at[call, o], recv.at[call, mine], peer(o)[1]).wait_send()
        total = buffer[call, 0]
        for i in range(1, n):
            total = total + buffer[call, i]
        return total

    def reduce_start(call, count):
        total = jnp.sum(dots[...], axis=1)
        column = jnp.sum(total, axis=1, keepdims=True)
        lane = lax.broadcasted_iota(jnp.int32, (24, 128), 1)
        place = lax.broadcasted_iota(jnp.int32, (24, 128), 0)
        keep = (lane == place) & (place < count)
        reduce_send(call, 0, jnp.sum(jnp.where(keep, column, 0.0), axis=0, keepdims=True))

    def reduce_middle(call):
        reduce_send(call, 1, reduce_wait(call, 0))

    def reduce_end(call, count):
        total = reduce_wait(call, 1)
        return [jnp.broadcast_to(total[:, i : i + 1], (8, 128)) for i in range(count)]

    def peer_copies(snap):
        block = table.at[snap, pl.ds(pl.multiple_of(me * 8, 8), 8)]
        return [remote(block, block, peer_s.at[snap], peer_r.at[snap], core_peer(grp, dom, o)) for o in range(1, DOMS)]

    def wait_peers(snap):
        arrived = table.at[snap, pl.ds(0, 8 * (DOMS - 1))]
        copy = remote(arrived, arrived, peer_s.at[snap], peer_r.at[snap], core_peer(grp, dom, 1))
        copy.wait_recv()
        copy.wait_send()

    def core_block(snap, which):
        return table.at[snap, pl.ds(pl.multiple_of(which * 512, 512), 512)]

    def core_copy(snap):
        block = core_block(snap, grp)
        return remote(block, block, core_s.at[snap], core_r.at[snap], other_core)

    def wait_core(snap):
        block = core_block(snap, 1 - grp)
        remote(block, block, core_s.at[snap], core_r.at[snap], other_core).wait_recv()
        core_copy(snap).wait_send()

    def start_all(copies):
        for copy in copies:
            copy.start()

    def write_to(ref):
        def write(i, row):
            ref[i : i + 1, :] = row

        return write

    def first_copies():
        return [
            remote(ref.at[pl.ds(at, PLANE)], first.at[1 - side, i], first_s.at[side, i], first_r.at[1 - side, i], who)
            for side, at, _, who in sides
            for i, ref in enumerate((vel, mass))
        ]

    start_all(first_copies())
    for e in (0, 3, 1, 2):
        rows = pl.ds(e * 256, 256)
        store_inner(basis.at[0], vel, e, force[rows, :] - (1.0 / GAIN) * products(vel, e), -PENALTY)
    expand(0, True, (0, 3))
    exchange_send(0, 0)
    expand(0, True, (1, 2))
    onehot_rows(sample, hot_sample)
    for copy in first_copies():
        copy.wait()
    for side in range(2):
        outer(0, side, first[side, 0], -PENALTY)
    expand(0, True, (0, 3))
    for copy in exchange_copies(0):
        copy.wait()
    for side, at, _, _ in sides:
        own = basis[0, at : at + PLANE, :]
        given = PENALTY * vel[at : at + PLANE, :]
        mapped = edge_map(side, given)
        then = outer(1, side, ghost[0, side, 0] + given, 0.5 * pull)
        beside[side, 0] = ghost[0, side, 1] + 0.5 * mapped - (0.5 * pull) * own
        beside[side, 1] = (
            ghost[0, side, 2] + 0.5 * edge_map(side, mapped - pull * own) + (0.5 * REACH - 1.0) * given - pull * then
        )

    for step in range(STEPS):
        call = 2 * step
        if step > 0:
            expand(0, True, (0, 3))
            exchange_send(2 * step, 0)
            expand(0, True, (1, 2))
            picked = []
            pick(out[...], sample, hot_sample, lambda i, row: picked.append(row))
            table[step - 1, pl.ds(pl.multiple_of(me * 8, 8), 8), :] = jnp.concatenate(picked, axis=0)
            start_all(peer_copies(step - 1))
            exchange_wait(2 * step, 0, True)
        follow(1)
        index = {}
        for j in range(4):
            for i in range(min(j, 2) + 1):
                index[i, j] = index[j, i] = len(index) - sum(1 for a, b in index if a > b)
        accumulate([(n, i, j) for (i, j), n in index.items() if i <= j], 64)
        reduce_start(call, 9)
        expand(3, False, (0, 3))
        exchange_send(2 * step + 1, 3)
        expand(3, False, (1, 2))
        reduce_middle(call)
        if step == 0:
            onehot_rows(part, hot_part)
        exchange_wait(2 * step + 1, 3, False)
        follow(4)
        m = reduce_end(call, 9)
        gram = [[m[index[i, j]] for j in range(3)] for i in range(4)]
        image = image_rows(gram, 3)
        head = [[image[max(i, j)][min(i, j)] for j in range(3)] for i in range(3)]
        opening = solve(head, gram[0])
        after_three = [-c for c in image_coefs(opening)]
        after_three[0] = 1.0 + after_three[0]
        combos = [after_three, shifted(after_three)]
        for _ in range(2):
            combos.append([2.0 * c for c in shifted(combos[-1])])
            for i, c in enumerate(combos[-3]):
                combos[-1][i] = combos[-1][i] - c
        factors = [[wide(c) for c in coefs] for coefs in combos]
        pairs = [(i, 4 + j) for j in range(3) for i in range(4)]
        pairs += [(4 + i, 4 + j) for j in range(4) for i in range(min(j, 2) + 1)]

        def gather_dots(c, carry):
            at = pl.multiple_of(c * 16, 16)
            rows = [basis[s, pl.ds(at, 16), :] for s in range(7)]
            for coefs in factors:
                value = coefs[0] * rows[0]
                for c_i, row in zip(coefs[1:], rows[1:7]):
                    value = value + c_i * row
                rows.append(value)
            held = rows[:4] + rows[7:]
            return tuple(acc + fold(held[a] * held[b]) for acc, (a, b) in zip(carry, pairs))

        carry = lax.fori_loop(0, 64, gather_dots, tuple(jnp.zeros((8, 128), F32) for _ in pairs))
        for i, acc in enumerate(carry):
            dots[i] = acc
        reduce_start(call + 1, len(pairs))
        if step > 0:
            wait_peers(step - 1)
            core_copy(step - 1).start()
        reduce_middle(call + 1)
        if step > 0:
            wait_core(step - 1)
            pick(table[step - 1], part, hot_part, write_to(feats))
        m = reduce_end(call + 1, len(pairs))
        index = {}
        for n, (a, b) in enumerate(pairs):
            index[a, b] = index[b, a] = n
        cross = image_rows([[m[index[i, 4 + j]] for j in range(3)] for i in range(4)], 3)
        gram = [[m[index[4 + i, 4 + j]] for j in range(3)] for i in range(4)]
        image = image_rows(gram, 3)
        whole = [[None] * 6 for _ in range(6)]
        for i in range(3):
            for j in range(3):
                whole[i][j] = head[i][j]
                whole[3 + i][3 + j] = image[max(i, j)][min(i, j)]
                whole[i][3 + j] = whole[3 + j][i] = cross[i][j]
        coefs = solve(whole, [m[index[i, 4]] for i in range(3)] + gram[0])
        moves = merged([(None, opening), (None, coefs[:3])] + [(coefs[3 + j], combos[j]) for j in range(3)])
        lost = image_coefs(coefs[3:])
        rest = merged([(None, combos[0])] + [(-lost[j], combos[j]) for j in range(4)] + [(-1.0, image_coefs(coefs[:3]))])
        moves = [wide(c) for c in moves]
        rest = [wide(c) for c in rest]
        start = vel if step == 0 else out
        more = step < STEPS - 1

        def advance(c, carry):
            rows = pl.ds(pl.multiple_of(c * 16, 16), 16)
            held = [basis[s, rows, :] for s in range(7 if more else 6)]
            moved = moves[0] * held[0]
            for c_i, row in zip(moves[1:], held[1:]):
                moved = moved + c_i * row
            if more:
                value = mass[rows, :] * moved
                for c_i, row in zip(rest, held):
                    value = value + c_i * row
                basis[0, rows, :] = value
            out[rows, :] = start[rows, :] + moved
            return carry

        lax.fori_loop(0, 64, advance, 0, unroll=2)

    last = STEPS - 1
    picked = []
    pick(out[...], sample, hot_sample, lambda i, row: picked.append(row))
    table[last, pl.ds(pl.multiple_of(me * 8, 8), 8), :] = jnp.concatenate(picked, axis=0)
    start_all(peer_copies(last))
    wait_peers(last)
    core_copy(last).start()
    wait_core(last)
    pick(table[last], part, hot_part, write_to(target))


VMEM = pl.BlockSpec(memory_space=pltpu.VMEM)
SMEM = pl.BlockSpec(memory_space=pltpu.SMEM)
ANY = pl.BlockSpec(memory_space=pl.ANY)


def run_steps(velocity, forcing, mass, sample, part):
    dma = pltpu.SemaphoreType.DMA
    return pl.pallas_call(
        steps_kernel,
        out_shape=(
            jax.ShapeDtypeStruct((ROWS, 256), F32),
            jax.ShapeDtypeStruct((8, 256), F32),
            jax.ShapeDtypeStruct((8, 256), F32),
        ),
        in_specs=[VMEM] * 8,
        out_specs=(VMEM,) * 3,
        scratch_shapes=[
            pltpu.VMEM((7, ROWS, 256), F32),
            pltpu.VMEM((4, 2, 3, PLANE, 256), F32),
            pltpu.VMEM((4, 2, 3, PLANE, 256), F32),
            pltpu.VMEM((2, 2, PLANE, 256), F32),
            pltpu.VMEM((2, 2, PLANE, 256), F32),
            pltpu.VMEM((24, 8, 128), F32),
            pltpu.VMEM((4, 8, 8, 128), F32),
            pltpu.VMEM((4, 16, 8, 128), F32),
            pltpu.VMEM((2, ROWS, 256), F32),
            pltpu.VMEM((ROWS, NODES), BF16),
            pltpu.VMEM((ROWS, NODES), BF16),
            dma((4, 2)), dma((4, 2)),
            dma((2, 2)), dma((2, 2)),
            dma((4, 8)), dma((4, 8)),
            dma((4, 16)), dma((4, 16)),
            dma((2,)), dma((2,)),
            dma((2,)), dma((2,)),
        ],
        compiler_params=pltpu.CompilerParams(
            collective_id=0, has_side_effects=True, vmem_limit_bytes=56 << 20
        ),
        cost_estimate=pl.CostEstimate(flops=30_000_000_000, bytes_accessed=4 << 20, transcendentals=0),
        name="viscous_steps",
    )(velocity, forcing, mass, sample, part, *field_matrices())


def split3(value, axis):
    high, low = split(value)
    return jnp.concatenate([high, high, low], axis=axis)


def split3_other(value, axis):
    high, low = split(value)
    return jnp.concatenate([high, low, high], axis=axis)


HALF_PAGES = 8
COUNT_ROWS = HALF_PAGES * NODES


def count_edges(key_ref, adj, accs):
    def clear(i, carry):
        for acc in accs:
            acc[pl.ds(pl.multiple_of(i * 128, 128), 128), :] = jnp.zeros((128, 128), jnp.int32)
        return carry

    lax.fori_loop(0, COUNT_ROWS // 128, clear, 0)
    place = lax.broadcasted_iota(jnp.int32, (8, 128), 0) * 128 + lax.broadcasted_iota(jnp.int32, (8, 128), 1)
    stream = EDGES // len(accs)

    def add(i, carry):
        for u in range(8):
            keys = [key_ref[c * stream + i * 8 + u] for c in range(len(accs))]
            spots = [pl.ds(pl.multiple_of((k >> 11) * 8, 8), 8) for k in keys]
            held = [acc[spot, :] for acc, spot in zip(accs, spots)]
            for acc, spot, k, value in zip(accs, spots, keys, held):
                word = jnp.full((8, 128), k, jnp.int32)
                one = lax.shift_left(jnp.full((8, 128), 1, jnp.int32), (word >> 6) & 16)
                acc[spot, :] = value + jnp.where((word & 1023) == place, one, 0)
        return carry

    lax.fori_loop(0, stream // 8, add, 0)

    def total(i, carry):
        rows = pl.ds(pl.multiple_of(i * 128, 128), 128)
        value = accs[0][rows, :]
        for acc in accs[1:]:
            value = value + acc[rows, :]
        accs[0][rows, :] = value
        return carry

    lax.fori_loop(0, COUNT_ROWS // 128, total, 0, unroll=2)

    def halves(rows):
        value = accs[0][rows, :]
        return (value & 65535).astype(F32), (value >> 16).astype(F32)

    worst = jnp.zeros((128, 128), F32)
    for page in range(HALF_PAGES):

        def move(i, most):
            at = pl.multiple_of(i * 128, 128)
            for h, value in enumerate(halves(page_rows(at, page, 128))):
                low = value.astype(BF16)
                column = h * 1024 + page * 128
                adj[pl.ds(at, 128), column : column + 128] = low
                most = jnp.maximum(most, jnp.abs(value - low.astype(F32)))
            return most

        worst = lax.fori_loop(0, NODES // 128, move, worst, unroll=2)
    flagged = jnp.max(worst) > 0.0

    @pl.when(flagged)
    def _():
        def keep(i, carry):
            rows = pl.ds(pl.multiple_of(i * 128, 128), 128)
            for acc, value in zip(accs, halves(rows)):
                acc[rows, :] = (value - value.astype(BF16).astype(F32)).astype(jnp.int32)
            return carry

        lax.fori_loop(0, COUNT_ROWS // 128, keep, 0)

    return flagged


def page_rows(start, page, count):
    return pl.ds(start * 8 + page, count, stride=8)


def surrogate_kernel(
    key_ref, feats, target, w_in_ref, b_in_ref, bias_ref, w_out_ref, weights, field,
    out, field_out,
    one, two, three, four, adj, feat_row, target_row, joined, slope, partial, sent, extra, grads, w_fwd, w_bwd, sem,
):
    tiles = NODES // 256
    field_copy = pltpu.make_async_copy(field, field_out, sem)
    field_copy.start()
    accs = (one, two, three, four)
    flagged = count_edges(key_ref, adj, accs)
    for i in range(8):
        feat_row[:, i * 256 : (i + 1) * 256] = feats[i : i + 1, :]
        target_row[:, i * 256 : (i + 1) * 256] = target[i : i + 1, :]
    vectors = [w_in_ref[...], b_in_ref[...], bias_ref[...], w_out_ref[...], jnp.zeros((123, 128), F32)]
    columns = jnp.concatenate(vectors, axis=0).T
    w_in, b_in, w_out = columns[:, 0:1], columns[:, 1:2], columns[:, 4:5]
    biases = (columns[:, 2:3], columns[:, 3:4])
    for layer in range(LAYERS):
        weight = weights[layer]
        w_fwd[layer] = split3_other(weight.T, 1)
        w_bwd[layer] = split3_other(weight, 1)
    grads[...] = jnp.zeros_like(grads)
    extra[...] = jnp.zeros_like(extra)

    def lanes(j):
        return pl.ds(pl.multiple_of(j * 256, 256), 256)

    def send(slot, at, value):
        high, low = split(value)
        sent[slot, 0:128, at] = high
        sent[slot, 128:256, at] = low

    def both(rows):
        return rows[:128] + rows[128:]

    def spill(half, rows):
        return accs[half][rows, :].astype(F32).astype(BF16)

    def gather_extra(slot):
        @pl.when(flagged)
        def _():
            for half in range(2):

                def body(page, carry):
                    rows = both(mm(sent[slot], spill(half, page_rows(0, page, NODES))))
                    extra[:, pl.ds(pl.multiple_of(half * 1024 + page * 128, 128), 128)] = rows
                    return carry

                lax.fori_loop(0, HALF_PAGES, body, 0)

    def scatter_extra(slot):
        @pl.when(flagged)
        def _():
            def body(j, carry):
                rows = jnp.zeros((256, 256), F32)
                for half in range(2):
                    for page in range(HALF_PAGES):
                        column = half * 1024 + page * 128
                        block = spill(half, page_rows(j * 256, page, 256))
                        rows = rows + mm_lanes(sent[slot, :, column : column + 128], block)
                extra[:, lanes(j)] = both(rows)
                return carry

            lax.fori_loop(0, tiles, body, 0)

    def gather(slot, at):
        return AGG_SCALE * (both(mm(sent[slot], adj[:, at])) + extra[:, at])

    def scatter(slot, at):
        return AGG_SCALE * (both(mm_lanes(sent[slot], adj[at, :])) + extra[:, at])

    def opening(j, carry):
        at = lanes(j)
        value = jnp.tanh(w_in * feat_row[:, at] + b_in)
        joined[0, 0:128, at] = value
        send(0, at, value)
        return carry

    lax.fori_loop(0, tiles, opening, 0, unroll=2)

    def update(layer, at):
        joined[layer, 128:256, at] = gather(layer, at)
        bump = jnp.tanh(mm(w_fwd[layer], split3(joined[layer, :, at], 0)) + biases[layer])
        slope[layer, :, at] = 1.0 - bump * bump
        return joined[layer, 0:128, at] + bump

    def back(layer, at, above):
        pre = above * slope[layer, :, at]
        spot = slice(layer * 256, layer * 256 + 256)
        grads[spot, :] = grads[spot, :] + mm_lanes(split3(joined[layer, :, at], 1), split3_other(pre, 1))
        below = mm(w_bwd[layer], split3(pre, 0))
        partial[layer, :, at] = above + below[:128]
        send(2 + layer, at, below[128:])
        return jnp.sum(pre, axis=1, keepdims=True)

    def second(j, carry):
        at = lanes(j)
        value = update(0, at)
        joined[1, 0:128, at] = value
        send(1, at, value)
        return carry

    gather_extra(0)
    lax.fori_loop(0, tiles, second, 0, unroll=8)

    zero = jnp.zeros((128, 1), F32)

    def third(j, carry):
        loss, grad_out, grad_bias = carry
        at = lanes(j)
        value = update(1, at)
        miss = jnp.sum(w_out * value, axis=0, keepdims=True) - target_row[:, at]
        scaled = miss * (2.0 / (NODES * GROUPS * DOMS))
        loss = loss + miss * miss
        grad_out = grad_out + jnp.sum(value * scaled, axis=1, keepdims=True)
        return loss, grad_out, grad_bias + back(1, at, w_out * scaled)

    gather_extra(1)
    loss, grad_out, bias_1 = lax.fori_loop(
        0, tiles, third, (jnp.zeros((1, 256), F32), zero, zero), unroll=8
    )

    def fourth(j, carry):
        at = lanes(j)
        return carry + back(0, at, partial[1, :, at] + scatter(3, at))

    scatter_extra(3)
    bias_0 = lax.fori_loop(0, tiles, fourth, zero, unroll=8)

    def fifth(j, carry):
        grad_in, grad_bias = carry
        at = lanes(j)
        value = joined[0, 0:128, at]
        pre = (partial[0, :, at] + scatter(2, at)) * (1.0 - value * value)
        grad_in = grad_in + jnp.sum(pre * feat_row[:, at], axis=1, keepdims=True)
        return grad_in, grad_bias + jnp.sum(pre, axis=1, keepdims=True)

    scatter_extra(2)
    grad_in, grad_bias = lax.fori_loop(0, tiles, fifth, (zero, zero), unroll=8)
    loss = jnp.sum(loss, axis=1, keepdims=True) * (1.0 / (NODES * GROUPS * DOMS))
    lane = lax.broadcasted_iota(jnp.int32, (128, 128), 1)
    packed = jnp.where(lane == 5, loss, 0.0)
    for i, column in enumerate((grad_in, grad_bias, bias_0, bias_1, grad_out)):
        packed = packed + jnp.where(lane == i, column, 0.0)
    blank = jnp.zeros((3, 128), F32)
    for f in range(128):
        out[f, 0:4, :] = grads[4 * f : 4 * f + 4, :]
        out[f, 4:5, :] = packed[f : f + 1, :]
        out[f, 5:8, :] = blank
    field_copy.wait()


def surrogate(key, feats, target, w_in, b_in, layer_bias, w_out, layer_weights, field):
    return pl.pallas_call(
        surrogate_kernel,
        out_shape=(jax.ShapeDtypeStruct((128, 8, 128), F32), jax.ShapeDtypeStruct((ROWS, 256), F32)),
        in_specs=[SMEM] + [VMEM] * 7 + [ANY],
        out_specs=(VMEM, ANY),
        scratch_shapes=[pltpu.VMEM((COUNT_ROWS + 8, 128), jnp.int32)] * 4
        + [
            pltpu.VMEM((NODES, NODES), BF16),
            pltpu.VMEM((1, NODES), F32),
            pltpu.VMEM((1, NODES), F32),
            pltpu.VMEM((LAYERS, 256, NODES), F32),
            pltpu.VMEM((LAYERS, 128, NODES), F32),
            pltpu.VMEM((LAYERS, 128, NODES), F32),
            pltpu.VMEM((4, 256, NODES), BF16),
            pltpu.VMEM((128, NODES), F32),
            pltpu.VMEM((LAYERS * 256, 128), F32),
            pltpu.VMEM((LAYERS, 128, 768), BF16),
            pltpu.VMEM((LAYERS, 256, 384), BF16),
            pltpu.SemaphoreType.DMA,
        ],
        compiler_params=pltpu.CompilerParams(vmem_limit_bytes=61 << 20),
        name="surrogate",
    )(
        key, feats, target, w_in.reshape(1, 128), b_in.reshape(1, 128), layer_bias, w_out.reshape(1, 128),
        layer_weights, field,
    )


def edge_keys(source, target_node, valid):
    return jnp.where(valid != 0, source * NODES + target_node, NODES * NODES).astype(jnp.int32)


def sum_kernel(
    grads, out, other, total, share, result, core_s, core_r, share_s, share_r, back_s, back_r, last_s, last_r
):
    grp = lax.axis_index("grp")
    dom = lax.axis_index("dom")
    other_core = (1 - grp, dom)
    peers = [core_peer(grp, dom, o) for o in range(1, DOMS)]

    def remote(src, dst, send, recv, who):
        return pltpu.make_async_remote_copy(
            src_ref=src, dst_ref=dst, send_sem=send, recv_sem=recv, device_id=who, device_id_type=MESH
        )

    barrier = pltpu.get_barrier_semaphore()
    for who in peers + [other_core]:
        pl.semaphore_signal(barrier, inc=1, device_id=who, device_id_type=MESH)
    pl.semaphore_wait(barrier, DOMS)

    def half(which):
        return pl.ds(pl.multiple_of(which * DOMS, DOMS), DOMS)

    copy = remote(grads.at[half(1 - grp)], other, core_s, core_r, other_core)
    copy.start()
    copy.wait()
    total[...] = grads[half(grp)] + other[...]
    for _, peer in peers:
        remote(total.at[peer], share.at[dom], share_s, share_r, (grp, peer)).start()
    share[dom] = total[dom]
    arrived = share.at[pl.ds(0, DOMS - 1)]
    copy = remote(arrived, arrived, share_s, share_r, peers[0])
    copy.wait_recv()
    copy.wait_send()
    parts = [share[i] for i in range(DOMS)]
    while len(parts) > 1:
        parts = [a + b for a, b in zip(parts[::2], parts[1::2])]
    mine = grp * DOMS + dom
    result[mine] = parts[0]
    for who in peers:
        remote(result.at[mine], result.at[mine], back_s, back_r, who).start()
    arrived = result.at[pl.ds(0, DOMS - 1)]
    copy = remote(arrived, arrived, back_s, back_r, peers[0])
    copy.wait_recv()
    copy.wait_send()
    own = result.at[half(grp)]
    copy = remote(own, own, last_s, last_r, other_core)
    copy.start()
    out[half(grp)] = result[half(grp)]
    there = result.at[half(1 - grp)]
    remote(there, there, last_s, last_r, other_core).wait_recv()
    out[half(1 - grp)] = result[half(1 - grp)]
    copy.wait_send()


def sum_grads(grads):
    dma = pltpu.SemaphoreType.DMA
    return pl.pallas_call(
        sum_kernel,
        out_shape=jax.ShapeDtypeStruct((128, 8, 128), F32),
        in_specs=[VMEM],
        out_specs=VMEM,
        scratch_shapes=[
            pltpu.VMEM((DOMS, 8, 128), F32),
            pltpu.VMEM((DOMS, 8, 128), F32),
            pltpu.VMEM((DOMS, 8, 128), F32),
            pltpu.VMEM((2 * DOMS, 8, 128), F32),
        ]
        + [dma] * 8,
        compiler_params=pltpu.CompilerParams(collective_id=1, has_side_effects=True, vmem_limit_bytes=32 << 20),
        name="sum_grads",
    )(grads)


def unpack_kernel(tiles, weight_out, in_out, bias_in_out, bias_out, head_out, loss_out):
    for f in range(128):
        weight_out[f // 64, f % 64 * 4 : f % 64 * 4 + 4, :] = tiles[f, 0:4, :]
    rows = tiles[:, 4, :].T
    in_out[...] = rows[0:1, :]
    bias_in_out[...] = rows[1:2, :]
    bias_out[...] = rows[2:4, :]
    head_out[...] = rows[4:5, :]
    loss_out[...] = rows[5:6, 0:1]


def unpack(tiles):
    row = jax.ShapeDtypeStruct((1, 128), F32)
    return pl.pallas_call(
        unpack_kernel,
        out_shape=(
            jax.ShapeDtypeStruct((LAYERS, 256, 128), F32), row, row, jax.ShapeDtypeStruct((2, 128), F32), row,
            jax.ShapeDtypeStruct((1, 1), F32),
        ),
        in_specs=[VMEM],
        out_specs=(VMEM,) * 6,
        name="unpack",
    )(tiles)


def shards(
    velocity, forcing, mass, sample_index, partition, edge_source, edge_target, edge_valid,
    w_in, b_in, layer_weights, layer_bias, w_out,
):
    shape = velocity.shape
    field, feats, target = run_steps(
        velocity.reshape(ROWS, 256), forcing.reshape(ROWS, 256), mass.reshape(ROWS, 256),
        sample_index.reshape(16, 128), partition.reshape(16, 128),
    )
    grads, field = surrogate(
        edge_keys(edge_source, edge_target, edge_valid), feats, target, w_in, b_in, layer_bias, w_out, layer_weights,
        field,
    )
    weight, grad_in, grad_bin, bias, head, loss = unpack(sum_grads(grads))
    return (
        field.reshape(shape), loss.reshape(()), grad_in.reshape(128), grad_bin.reshape(128), weight, bias,
        head.reshape(128),
    )


def solution(mesh):
    many = P(("grp", "dom"))
    block = P(("grp", "dom"), None, None)
    return jax.shard_map(
        shards,
        mesh=mesh,
        in_specs=(block,) * 3 + (many,) * 5 + (P(),) * 5,
        out_specs=(block,) + (P(),) * 6,
        check_vma=False,
    )
```

time: 2300 us -> 179 us (0.08)
  blocking collectives: 1440 us -> 0 us
  other arithmetic: 364 us -> 1.41 us
  waiting for transfers between devices: 177 us -> 0 us
  Pallas kernels: 0 us -> 172 us
  matrix products: 118 us -> 0 us
  local copies, waits for them, and re-layouts: 88.1 us -> 1.83 us
  starting transfers between devices: 46.5 us -> 0 us
  between operations: 46.1 us -> 0.9 us
    psum x23 -> x0, blocking collectives: 1440 us -> none  [the longest x12 759 us: squares(): return lax.psum(jnp.sum(residual * residual), ('grp', 'dom'))]
    scatter-add x4 -> x0, other arithmetic: 308 us -> none  [the longest x2 167 us: propagate(): carried = state[source] * valid[:, None].astype(jnp.float32)]
    pallas_call x0 -> x4, Pallas kernels: none -> 172 us  [the longest x1 96 us: run_steps(): pl.pallas_call(steps_kernel, out_shape=(jax.ShapeDtypeStruct((ROWS, 256),...]
    dot_general x50 -> x0, matrix products: 118 us -> none  [the longest x14 56.6 us: operate(): jnp.einsum('ij,jyz->iyz', stream_mat, field, precision=lax.Precision.HIGH...]
    ppermute x28 -> x0, waiting for transfers between devices: 115 us -> none  [the longest x14 103 us: with_halo(): lax.ppermute(lax.slice_in_dim(block, block.shape[dim] - width, None, axis...]
    all_gather x1 -> x0, waiting for transfers between devices: 61.2 us -> none  [shards(): lax.all_gather(jnp.stack(samples), ('grp', 'dom'), axis=1, tiled=True)]
    gather x4 -> x0, local copies, waits for them, and re-layouts: 59.8 us -> none  [the longest x2 36.3 us: shards(): samples.append(field.reshape(-1)[sample_index])]
    ppermute x28 -> x0, starting transfers between devices: 46.5 us -> none  [the longest x14 43.2 us: with_halo(): lax.ppermute(lax.slice_in_dim(block, 0, width, axis=dim), axis, backward)]
  transfers between devices with their start and end apart: 30 -> 0, of which waited for: 29 -> 0; matrix products, arithmetic and copies ran while one was open for 4% -> 0% of each run, Pallas kernels for 0% -> 0%
where the time goes in v1:
time: 179 us; the launch traced here: 176 us
  Pallas kernels  172 us (96%)
  local copies, waits for them, and re-layouts  1.83 us (1%)
    pallas_call x1, Pallas kernels, run_steps(): pl.pallas_call(steps_kernel, out_shape=(jax.ShapeDtypeStruct((ROWS, 256),...  96 us
    pallas_call x1, Pallas kernels, surrogate(): pl.pallas_call(surrogate_kernel, out_shape=(jax.ShapeDtypeStruct((128, 8,...  52.7 us
    pallas_call x1, Pallas kernels, sum_grads(): pl.pallas_call(sum_kernel, out_shape=jax.ShapeDtypeStruct((128, 8, 128),...  21.6 us

profile of v1, /device:TPU:1, one launch (start us, length us, event | category | flops | bytes accessed | tf_op | source)
XLA Modules:
  0.0 176.2 jit_solution(10290589281917364301)
XLA Ops:
  0.6 1.4 add_select_fusion.key_ref
  2.0 96.0 %viscous_steps.1 = (f32[1024,256]{1,0:T(8,128)}, f32[8,256]{1,0:T(8,128)}, f32[8,256]{1,0:T(8,128)}) custom-call(f32[1024,256]{1,0:T(8,128)} %bitcast.16, f32[1024,256]{1,0:T(8,128)} %bitcast.17, f32[1024,256]{1,0:T(8,128)} %bitcast.18, s32[16,128]{1,0:T(8,128)} %bitcast.20, s32[16,128]{1,0:T(8,128)} %bitcast.21, bf16[256,768]{1,0:T(8,128)(2,1)} %constant.12.clone.left_mat, ...), custom_call_target="tpu_custom_call" | custom-call | flops 30000001024 | bytes 4194304 | tf_op jit(solution)/shard_map/viscous_steps/pallas_call | solution.py:564
  98.1 52.7 %surrogate.1 = (f32[128,8,128]{2,1,0:T(8,128)}, f32[1024,256]{1,0:T(8,128)}) custom-call(s32[8192]{0:T(1024)} %add_select_fusion.key_ref, f32[8,256]{1,0:T(8,128)} %get-tuple-element.18.feats, f32[8,256]{1,0:T(8,128)} %get-tuple-element.19.target, f32[1,128]{1,0:T(1,128)} %bitcast.13, f32[1,128]{1,0:T(1,128)} %bitcast.14, f32[2,128]{1,0:T(2,128)} %bias_ref.1, ...), custom_call_target="tpu_custom_call" | custom-call | tf_op jit(solution)/shard_map/surrogate/pallas_call | solution.py:836
  150.7 0.0 copy-start.1
  150.8 1.0 copy-done.1
  151.8 21.6 %sum_grads.1.tiles = f32[128,8,128]{2,1,0:T(8,128)S(1)} custom-call(f32[128,8,128]{2,1,0:T(8,128)S(1)} %copy-done.1), custom_call_target="tpu_custom_call" | custom-call | tf_op jit(solution)/shard_map/sum_grads/pallas_call | solution.py:923
  173.4 0.0 copy-start
  173.4 0.8 copy-done
  174.2 1.8 %unpack.1 = (f32[2,256,128]{2,1,0:T(8,128)}, f32[1,128]{1,0:T(1,128)}, f32[1,128]{1,0:T(1,128)}, f32[2,128]{1,0:T(2,128)}, f32[1,128]{1,0:T(1,128)}, /*index=5*/f32[1,1]{1,0:T(1,128)}) custom-call(f32[128,8,128]{2,1,0:T(8,128)} %copy-done), custom_call_target="tpu_custom_call" | custom-call | tf_op jit(solution)/shard_map/unpack/pallas_call | solution.py:953
Async XLA Ops:
  150.7 1.0 copy-start.1
  173.4 0.8 copy-start

commit v2 on v1

--- a/solution.py
+++ b/solution.py
@@ -203,8 +203,8 @@
 
 
 def steps_kernel(
-    vel, force, mass, sample, part, left_mat, right_mat, edge_mat,
-    out, feats, target,
+    vel, force, mass, sample, part, source, target_node, valid, left_mat, right_mat, edge_mat,
+    out, feats, target, keys,
     basis, stage, ghost, first, beside, dots, near, far, table, hot_sample, hot_part,
     halo_s, halo_r, first_s, first_r, near_s, near_r, far_s, far_r, peer_s, peer_r, core_s, core_r,
 ):
@@ -235,7 +235,6 @@
     greeted += [after_id, before_id]
     for who in greeted:
         pl.semaphore_signal(barrier, inc=1, device_id=who, device_id_type=MESH)
-    pl.semaphore_wait(barrier, len(greeted))
 
     def remote(src, dst, send, recv, who):
         return pltpu.make_async_remote_copy(
@@ -416,14 +415,16 @@
             for i, ref in enumerate((vel, mass))
         ]
 
-    start_all(first_copies())
     for e in (0, 3, 1, 2):
         rows = pl.ds(e * 256, 256)
         store_inner(basis.at[0], vel, e, force[rows, :] - (1.0 / GAIN) * products(vel, e), -PENALTY)
     expand(0, True, (0, 3))
+    pl.semaphore_wait(barrier, len(greeted))
+    start_all(first_copies())
     exchange_send(0, 0)
     expand(0, True, (1, 2))
     onehot_rows(sample, hot_sample)
+    keys[...] = jnp.where(valid[...] != 0, source[...] * NODES + target_node[...], NODES * NODES)
     for copy in first_copies():
         copy.wait()
     for side in range(2):
@@ -550,8 +551,14 @@
     start_all(peer_copies(last))
     wait_peers(last)
     core_copy(last).start()
+    here, there = (pl.ds(pl.multiple_of(which * 512, 512), 512) for which in (grp, 1 - grp))
+    pick(table[last, here, :], part, hot_part.at[here], write_to(target))
     wait_core(last)
-    pick(table[last], part, hot_part, write_to(target))
+
+    def add_to(i, row):
+        target[i : i + 1, :] = target[i : i + 1, :] + row
+
+    pick(table[last, there, :], part, hot_part.at[there], add_to)
 
 
 VMEM = pl.BlockSpec(memory_space=pltpu.VMEM)
@@ -559,7 +566,7 @@
 ANY = pl.BlockSpec(memory_space=pl.ANY)
 
 
-def run_steps(velocity, forcing, mass, sample, part):
+def run_steps(velocity, forcing, mass, sample, part, source, target_node, valid):
     dma = pltpu.SemaphoreType.DMA
     return pl.pallas_call(
         steps_kernel,
@@ -567,9 +574,10 @@
             jax.ShapeDtypeStruct((ROWS, 256), F32),
             jax.ShapeDtypeStruct((8, 256), F32),
             jax.ShapeDtypeStruct((8, 256), F32),
+            jax.ShapeDtypeStruct((64, 128), jnp.int32),
         ),
-        in_specs=[VMEM] * 8,
-        out_specs=(VMEM,) * 3,
+        in_specs=[VMEM] * 11,
+        out_specs=(VMEM,) * 4,
         scratch_shapes=[
             pltpu.VMEM((7, ROWS, 256), F32),
             pltpu.VMEM((4, 2, 3, PLANE, 256), F32),
@@ -594,7 +602,7 @@
         ),
         cost_estimate=pl.CostEstimate(flops=30_000_000_000, bytes_accessed=4 << 20, transcendentals=0),
         name="viscous_steps",
-    )(velocity, forcing, mass, sample, part, *field_matrices())
+    )(velocity, forcing, mass, sample, part, source, target_node, valid, *field_matrices())
 
 
 def split3(value, axis):
@@ -683,13 +691,19 @@
 def surrogate_kernel(
     key_ref, feats, target, w_in_ref, b_in_ref, bias_ref, w_out_ref, weights, field,
     out, field_out,
-    one, two, three, four, adj, feat_row, target_row, joined, slope, partial, sent, extra, grads, w_fwd, w_bwd, sem,
+    one, two, three, four, adj, feat_row, target_row, state_0, state_1, agg_0, agg_1, slope_0, slope_1, partial_0, partial_1,
+    sent_0, sent_1, sent_2, sent_3, back_agg, extra, grads_0, grads_1, w_fwd, w_bwd, field_hold, sem,
 ):
     tiles = NODES // 256
-    field_copy = pltpu.make_async_copy(field, field_out, sem)
-    field_copy.start()
+    states, aggs, slopes, partials = (state_0, state_1), (agg_0, agg_1), (slope_0, slope_1), (partial_0, partial_1)
+    sent, grads = (sent_0, sent_1, sent_2, sent_3), (grads_0, grads_1)
+    field_in = pltpu.make_async_copy(field, field_hold, sem.at[0])
+    field_in.start()
     accs = (one, two, three, four)
     flagged = count_edges(key_ref, adj, accs)
+    field_in.wait()
+    field_back = pltpu.make_async_copy(field_hold, field_out, sem.at[1])
+    field_back.start()
     for i in range(8):
         feat_row[:, i * 256 : (i + 1) * 256] = feats[i : i + 1, :]
         target_row[:, i * 256 : (i + 1) * 256] = target[i : i + 1, :]
@@ -701,7 +715,8 @@
         weight = weights[layer]
         w_fwd[layer] = split3_other(weight.T, 1)
         w_bwd[layer] = split3_other(weight, 1)
-    grads[...] = jnp.zeros_like(grads)
+    for ref in grads:
+        ref[...] = jnp.zeros_like(ref)
     extra[...] = jnp.zeros_like(extra)
 
     def lanes(j):
@@ -709,8 +724,8 @@
 
     def send(slot, at, value):
         high, low = split(value)
-        sent[slot, 0:128, at] = high
-        sent[slot, 128:256, at] = low
+        sent[slot][0:128, at] = high
+        sent[slot][128:256, at] = low
 
     def both(rows):
         return rows[:128] + rows[128:]
@@ -724,7 +739,7 @@
             for half in range(2):
 
                 def body(page, carry):
-                    rows = both(mm(sent[slot], spill(half, page_rows(0, page, NODES))))
+                    rows = both(mm(sent[slot][...], spill(half, page_rows(0, page, NODES))))
                     extra[:, pl.ds(pl.multiple_of(half * 1024 + page * 128, 128), 128)] = rows
                     return carry
 
@@ -739,50 +754,65 @@
                     for page in range(HALF_PAGES):
                         column = half * 1024 + page * 128
                         block = spill(half, page_rows(j * 256, page, 256))
-                        rows = rows + mm_lanes(sent[slot, :, column : column + 128], block)
+                        rows = rows + mm_lanes(sent[slot][:, column : column + 128], block)
                 extra[:, lanes(j)] = both(rows)
                 return carry
 
             lax.fori_loop(0, tiles, body, 0)
 
-    def gather(slot, at):
-        return AGG_SCALE * (both(mm(sent[slot], adj[:, at])) + extra[:, at])
-
-    def scatter(slot, at):
-        return AGG_SCALE * (both(mm_lanes(sent[slot], adj[at, :])) + extra[:, at])
+    def gather(slot, into):
+        gather_extra(slot)
+
+        def body(j, carry):
+            at = lanes(j)
+            into[:, at] = AGG_SCALE * (both(mm(sent[slot][...], adj[:, at])) + extra[:, at])
+            return carry
+
+        lax.fori_loop(0, tiles, body, 0, unroll=8)
+
+    def scatter(slot):
+        scatter_extra(slot)
+
+        def body(j, carry):
+            at = lanes(j)
+            back_agg[:, at] = AGG_SCALE * (both(mm_lanes(sent[slot][...], adj[at, :])) + extra[:, at])
+            return carry
+
+        lax.fori_loop(0, tiles, body, 0, unroll=8)
 
     def opening(j, carry):
         at = lanes(j)
         value = jnp.tanh(w_in * feat_row[:, at] + b_in)
-        joined[0, 0:128, at] = value
+        states[0][:, at] = value
         send(0, at, value)
         return carry
 
     lax.fori_loop(0, tiles, opening, 0, unroll=2)
 
+    def joined(layer, at):
+        return jnp.concatenate([states[layer][:, at], aggs[layer][:, at]], axis=0)
+
     def update(layer, at):
-        joined[layer, 128:256, at] = gather(layer, at)
-        bump = jnp.tanh(mm(w_fwd[layer], split3(joined[layer, :, at], 0)) + biases[layer])
-        slope[layer, :, at] = 1.0 - bump * bump
-        return joined[layer, 0:128, at] + bump
+        bump = jnp.tanh(mm(w_fwd[layer], split3(joined(layer, at), 0)) + biases[layer])
+        slopes[layer][:, at] = 1.0 - bump * bump
+        return states[layer][:, at] + bump
 
     def back(layer, at, above):
-        pre = above * slope[layer, :, at]
-        spot = slice(layer * 256, layer * 256 + 256)
-        grads[spot, :] = grads[spot, :] + mm_lanes(split3(joined[layer, :, at], 1), split3_other(pre, 1))
+        pre = above * slopes[layer][:, at]
+        grads[layer][...] = grads[layer][...] + mm_lanes(split3(joined(layer, at), 1), split3_other(pre, 1))
         below = mm(w_bwd[layer], split3(pre, 0))
-        partial[layer, :, at] = above + below[:128]
+        partials[layer][:, at] = above + below[:128]
         send(2 + layer, at, below[128:])
         return jnp.sum(pre, axis=1, keepdims=True)
 
     def second(j, carry):
         at = lanes(j)
         value = update(0, at)
-        joined[1, 0:128, at] = value
+        states[1][:, at] = value
         send(1, at, value)
         return carry
 
-    gather_extra(0)
+    gather(0, agg_0)
     lax.fori_loop(0, tiles, second, 0, unroll=8)
 
     zero = jnp.zeros((128, 1), F32)
@@ -797,27 +827,27 @@
         grad_out = grad_out + jnp.sum(value * scaled, axis=1, keepdims=True)
         return loss, grad_out, grad_bias + back(1, at, w_out * scaled)
 
-    gather_extra(1)
+    gather(1, agg_1)
     loss, grad_out, bias_1 = lax.fori_loop(
         0, tiles, third, (jnp.zeros((1, 256), F32), zero, zero), unroll=8
     )
 
     def fourth(j, carry):
         at = lanes(j)
-        return carry + back(0, at, partial[1, :, at] + scatter(3, at))
-
-    scatter_extra(3)
+        return carry + back(0, at, partials[1][:, at] + back_agg[:, at])
+
+    scatter(3)
     bias_0 = lax.fori_loop(0, tiles, fourth, zero, unroll=8)
 
     def fifth(j, carry):
         grad_in, grad_bias = carry
         at = lanes(j)
-        value = joined[0, 0:128, at]
-        pre = (partial[0, :, at] + scatter(2, at)) * (1.0 - value * value)
+        value = states[0][:, at]
+        pre = (partials[0][:, at] + back_agg[:, at]) * (1.0 - value * value)
         grad_in = grad_in + jnp.sum(pre * feat_row[:, at], axis=1, keepdims=True)
         return grad_in, grad_bias + jnp.sum(pre, axis=1, keepdims=True)
 
-    scatter_extra(2)
+    scatter(2)
     grad_in, grad_bias = lax.fori_loop(0, tiles, fifth, (zero, zero), unroll=8)
     loss = jnp.sum(loss, axis=1, keepdims=True) * (1.0 / (NODES * GROUPS * DOMS))
     lane = lax.broadcasted_iota(jnp.int32, (128, 128), 1)
@@ -826,10 +856,10 @@
         packed = packed + jnp.where(lane == i, column, 0.0)
     blank = jnp.zeros((3, 128), F32)
     for f in range(128):
-        out[f, 0:4, :] = grads[4 * f : 4 * f + 4, :]
+        out[f, 0:4, :] = grads[f // 64][f % 64 * 4 : f % 64 * 4 + 4, :]
         out[f, 4:5, :] = packed[f : f + 1, :]
         out[f, 5:8, :] = blank
-    field_copy.wait()
+    field_back.wait()
 
 
 def surrogate(key, feats, target, w_in, b_in, layer_bias, w_out, layer_weights, field):
@@ -843,26 +873,23 @@
             pltpu.VMEM((NODES, NODES), BF16),
             pltpu.VMEM((1, NODES), F32),
             pltpu.VMEM((1, NODES), F32),
-            pltpu.VMEM((LAYERS, 256, NODES), F32),
-            pltpu.VMEM((LAYERS, 128, NODES), F32),
-            pltpu.VMEM((LAYERS, 128, NODES), F32),
-            pltpu.VMEM((4, 256, NODES), BF16),
-            pltpu.VMEM((128, NODES), F32),
-            pltpu.VMEM((LAYERS * 256, 128), F32),
+        ]
+        + [pltpu.VMEM((128, NODES), F32)] * 8
+        + [pltpu.VMEM((256, NODES), BF16)] * 4
+        + [pltpu.VMEM((128, NODES), F32)] * 2
+        + [pltpu.VMEM((256, 128), F32)] * 2
+        + [
             pltpu.VMEM((LAYERS, 128, 768), BF16),
             pltpu.VMEM((LAYERS, 256, 384), BF16),
-            pltpu.SemaphoreType.DMA,
+            pltpu.VMEM((ROWS, 256), F32),
+            pltpu.SemaphoreType.DMA((2,)),
         ],
-        compiler_params=pltpu.CompilerParams(vmem_limit_bytes=61 << 20),
+        compiler_params=pltpu.CompilerParams(vmem_limit_bytes=62 << 20),
         name="surrogate",
     )(
         key, feats, target, w_in.reshape(1, 128), b_in.reshape(1, 128), layer_bias, w_out.reshape(1, 128),
         layer_weights, field,
     )
-
-
-def edge_keys(source, target_node, valid):
-    return jnp.where(valid != 0, source * NODES + target_node, NODES * NODES).astype(jnp.int32)
 
 
 def sum_kernel(
@@ -967,13 +994,13 @@
     w_in, b_in, layer_weights, layer_bias, w_out,
 ):
     shape = velocity.shape
-    field, feats, target = run_steps(
+    field, feats, target, keys = run_steps(
         velocity.reshape(ROWS, 256), forcing.reshape(ROWS, 256), mass.reshape(ROWS, 256),
         sample_index.reshape(16, 128), partition.reshape(16, 128),
+        edge_source.reshape(64, 128), edge_target.reshape(64, 128), edge_valid.reshape(64, 128),
     )
     grads, field = surrogate(
-        edge_keys(edge_source, edge_target, edge_valid), feats, target, w_in, b_in, layer_bias, w_out, layer_weights,
-        field,
+        keys.reshape(EDGES), feats, target, w_in, b_in, layer_bias, w_out, layer_weights, field,
     )
     weight, grad_in, grad_bin, bias, head, loss = unpack(sum_grads(grads))
     return (

time: 179 us -> 166 us (0.927)
  Pallas kernels: 172 us -> 160 us
    pallas_call x1, Pallas kernels: 52.7 us -> 42.6 us  [surrogate(): pl.pallas_call(surrogate_kernel, out_shape=(jax.ShapeDtypeStruct((128, 8,...]
where the time goes in v2:
time: 166 us; the launch traced here: 163 us
  Pallas kernels  160 us (96%)
  local copies, waits for them, and re-layouts  1.83 us (1%)
    pallas_call x1, Pallas kernels, run_steps(): pl.pallas_call(steps_kernel, out_shape=(jax.ShapeDtypeStruct((ROWS, 256),...  94.3 us
    pallas_call x1, Pallas kernels, surrogate(): pl.pallas_call(surrogate_kernel, out_shape=(jax.ShapeDtypeStruct((128, 8,...  42.6 us
    pallas_call x1, Pallas kernels, sum_grads(): pl.pallas_call(sum_kernel, out_shape=jax.ShapeDtypeStruct((128, 8, 128),...  21.6 us

profile of v2, /device:TPU:1, one launch (start us, length us, event | category | flops | bytes accessed | tf_op | source)
XLA Modules:
  0.0 163.2 jit_solution(9780507256624728494)
XLA Ops:
  0.6 94.3 %viscous_steps.1 = (f32[1024,256]{1,0:T(8,128)}, f32[8,256]{1,0:T(8,128)}, f32[8,256]{1,0:T(8,128)}, s32[64,128]{1,0:T(8,128)}) custom-call(f32[1024,256]{1,0:T(8,128)} %bitcast.21, f32[1024,256]{1,0:T(8,128)} %bitcast.22, f32[1024,256]{1,0:T(8,128)} %bitcast.23, s32[16,128]{1,0:T(8,128)} %bitcast.28, s32[16,128]{1,0:T(8,128)} %bitcast.29, ...), custom_call_target="tpu_custom_call" | custom-call | flops 30000001024 | bytes 4194304 | tf_op jit(solution)/shard_map/viscous_steps/pallas_call | solution.py:571
  95.0 42.6 %surrogate.1 = (f32[128,8,128]{2,1,0:T(8,128)}, f32[1024,256]{1,0:T(8,128)}) custom-call(s32[8192]{0:T(1024)} %bitcast.17, f32[8,256]{1,0:T(8,128)} %get-tuple-element.20.feats, f32[8,256]{1,0:T(8,128)} %get-tuple-element.21.target, f32[1,128]{1,0:T(1,128)} %bitcast.18, f32[1,128]{1,0:T(1,128)} %bitcast.19, f32[2,128]{1,0:T(2,128)} %bias_ref.1, ...), custom_call_target="tpu_custom_call" | custom-call | tf_op jit(solution)/shard_map/surrogate/pallas_call | solution.py:866
  137.6 0.0 copy-start.1
  137.7 1.0 copy-done.1
  138.7 21.6 %sum_grads.1.tiles = f32[128,8,128]{2,1,0:T(8,128)S(1)} custom-call(f32[128,8,128]{2,1,0:T(8,128)S(1)} %copy-done.1), custom_call_target="tpu_custom_call" | custom-call | tf_op jit(solution)/shard_map/sum_grads/pallas_call | solution.py:950
  160.3 0.0 copy-start
  160.3 0.8 copy-done
  161.1 1.8 %unpack.1 = (f32[2,256,128]{2,1,0:T(8,128)}, f32[1,128]{1,0:T(1,128)}, f32[1,128]{1,0:T(1,128)}, f32[2,128]{1,0:T(2,128)}, f32[1,128]{1,0:T(1,128)}, /*index=5*/f32[1,1]{1,0:T(1,128)}) custom-call(f32[128,8,128]{2,1,0:T(8,128)} %copy-done), custom_call_target="tpu_custom_call" | custom-call | tf_op jit(solution)/shard_map/unpack/pallas_call | solution.py:980
Async XLA Ops:
  137.6 1.0 copy-start.1
  160.3 0.8 copy-start

commit v3 on v2

--- a/solution.py
+++ b/solution.py
@@ -203,9 +203,9 @@
 
 
 def steps_kernel(
-    vel, force, mass, sample, part, source, target_node, valid, left_mat, right_mat, edge_mat,
-    out, feats, target, keys,
-    basis, stage, ghost, first, beside, dots, near, far, table, hot_sample, hot_part,
+    vel, force_hbm, mass_hbm, sample, part, source, target_node, valid, left_mat, right_mat, edge_mat,
+    out_hbm, feats, target, keys,
+    force, mass, out, local, basis, stage, ghost, first, beside, dots, near, far, table, hot_sample, hot_part,
     halo_s, halo_r, first_s, first_r, near_s, near_r, far_s, far_r, peer_s, peer_r, core_s, core_r,
 ):
     grp = lax.axis_index("grp")
@@ -230,6 +230,12 @@
     after_id = (after // DOMS, after % DOMS)
     before_id = (before // DOMS, before % DOMS)
 
+    loads = [
+        pltpu.make_async_copy(force_hbm, force, local.at[0]),
+        pltpu.make_async_copy(mass_hbm, mass, local.at[1]),
+    ]
+    for copy in loads:
+        copy.start()
     barrier = pltpu.get_barrier_semaphore()
     greeted = [core_peer(grp, dom, o) for o in range(1, DOMS)] + [near_peer(o)[1] for o in range(1, 8)]
     greeted += [after_id, before_id]
@@ -415,6 +421,8 @@
             for i, ref in enumerate((vel, mass))
         ]
 
+    for copy in loads:
+        copy.wait()
     for e in (0, 3, 1, 2):
         rows = pl.ds(e * 256, 256)
         store_inner(basis.at[0], vel, e, force[rows, :] - (1.0 / GAIN) * products(vel, e), -PENALTY)
@@ -451,7 +459,6 @@
             picked = []
             pick(out[...], sample, hot_sample, lambda i, row: picked.append(row))
             table[step - 1, pl.ds(pl.multiple_of(me * 8, 8), 8), :] = jnp.concatenate(picked, axis=0)
-            start_all(peer_copies(step - 1))
             exchange_wait(2 * step, 0, True)
         follow(1)
         index = {}
@@ -466,6 +473,8 @@
         reduce_middle(call)
         if step == 0:
             onehot_rows(part, hot_part)
+        else:
+            start_all(peer_copies(step - 1))
         exchange_wait(2 * step + 1, 3, False)
         follow(4)
         m = reduce_end(call, 9)
@@ -545,6 +554,8 @@
         lax.fori_loop(0, 64, advance, 0, unroll=2)
 
     last = STEPS - 1
+    store = pltpu.make_async_copy(out, out_hbm, local.at[2])
+    store.start()
     picked = []
     pick(out[...], sample, hot_sample, lambda i, row: picked.append(row))
     table[last, pl.ds(pl.multiple_of(me * 8, 8), 8), :] = jnp.concatenate(picked, axis=0)
@@ -559,6 +570,7 @@
         target[i : i + 1, :] = target[i : i + 1, :] + row
 
     pick(table[last, there, :], part, hot_part.at[there], add_to)
+    store.wait()
 
 
 VMEM = pl.BlockSpec(memory_space=pltpu.VMEM)
@@ -576,9 +588,13 @@
             jax.ShapeDtypeStruct((8, 256), F32),
             jax.ShapeDtypeStruct((64, 128), jnp.int32),
         ),
-        in_specs=[VMEM] * 11,
-        out_specs=(VMEM,) * 4,
+        in_specs=[VMEM, ANY, ANY] + [VMEM] * 8,
+        out_specs=(ANY, VMEM, VMEM, VMEM),
         scratch_shapes=[
+            pltpu.VMEM((ROWS, 256), F32),
+            pltpu.VMEM((ROWS, 256), F32),
+            pltpu.VMEM((ROWS, 256), F32),
+            dma((3,)),
             pltpu.VMEM((7, ROWS, 256), F32),
             pltpu.VMEM((4, 2, 3, PLANE, 256), F32),
             pltpu.VMEM((4, 2, 3, PLANE, 256), F32),
@@ -893,7 +909,7 @@
 
 
 def sum_kernel(
-    grads, out, other, total, share, result, core_s, core_r, share_s, share_r, back_s, back_r, last_s, last_r
+    grads_hbm, out, grads, local, other, total, share, result, core_s, core_r, share_s, share_r, back_s, back_r, last_s, last_r
 ):
     grp = lax.axis_index("grp")
     dom = lax.axis_index("dom")
@@ -905,9 +921,12 @@
             src_ref=src, dst_ref=dst, send_sem=send, recv_sem=recv, device_id=who, device_id_type=MESH
         )
 
+    load = pltpu.make_async_copy(grads_hbm, grads, local)
+    load.start()
     barrier = pltpu.get_barrier_semaphore()
     for who in peers + [other_core]:
         pl.semaphore_signal(barrier, inc=1, device_id=who, device_id_type=MESH)
+    load.wait()
     pl.semaphore_wait(barrier, DOMS)
 
     def half(which):
@@ -950,16 +969,18 @@
     return pl.pallas_call(
         sum_kernel,
         out_shape=jax.ShapeDtypeStruct((128, 8, 128), F32),
-        in_specs=[VMEM],
+        in_specs=[ANY],
         out_specs=VMEM,
         scratch_shapes=[
+            pltpu.VMEM((2 * DOMS, 8, 128), F32),
+            dma,
             pltpu.VMEM((DOMS, 8, 128), F32),
             pltpu.VMEM((DOMS, 8, 128), F32),
             pltpu.VMEM((DOMS, 8, 128), F32),
             pltpu.VMEM((2 * DOMS, 8, 128), F32),
         ]
         + [dma] * 8,
-        compiler_params=pltpu.CompilerParams(collective_id=1, has_side_effects=True, vmem_limit_bytes=32 << 20),
+        compiler_params=pltpu.CompilerParams(collective_id=1, has_side_effects=True, vmem_limit_bytes=60 << 20),
         name="sum_grads",
     )(grads)
 
@@ -985,6 +1006,7 @@
         ),
         in_specs=[VMEM],
         out_specs=(VMEM,) * 6,
+        compiler_params=pltpu.CompilerParams(vmem_limit_bytes=60 << 20),
         name="unpack",
     )(tiles)
 

time: 166 us -> 168 us (1.012)
  Pallas kernels: 160 us -> 164 us
  local copies, waits for them, and re-layouts: 1.83 us -> 0 us
    pallas_call x1, Pallas kernels: 94.3 us -> 97.4 us  [run_steps(): pl.pallas_call(steps_kernel, out_shape=(jax.ShapeDtypeStruct((ROWS, 256),...]
    unnamed x4 -> x0, local copies, waits for them, and re-layouts: 1.83 us -> none
where the time goes in v3:
time: 168 us; the launch traced here: 165 us
  Pallas kernels  164 us (98%)
    pallas_call x1, Pallas kernels, run_steps(): pl.pallas_call(steps_kernel, out_shape=(jax.ShapeDtypeStruct((ROWS, 256),...  97.4 us
    pallas_call x1, Pallas kernels, surrogate(): pl.pallas_call(surrogate_kernel, out_shape=(jax.ShapeDtypeStruct((128, 8,...  42.6 us
    pallas_call x1, Pallas kernels, sum_grads(): pl.pallas_call(sum_kernel, out_shape=jax.ShapeDtypeStruct((128, 8, 128),...  22.6 us

profile of v3, /device:TPU:1, one launch (start us, length us, event | category | flops | bytes accessed | tf_op | source)
XLA Modules:
  0.0 165.2 jit_solution(9641092506971400069)
XLA Ops:
  0.6 97.4 %viscous_steps.1 = (f32[1024,256]{1,0:T(8,128)}, f32[8,256]{1,0:T(8,128)}, f32[8,256]{1,0:T(8,128)}, s32[64,128]{1,0:T(8,128)}) custom-call(f32[1024,256]{1,0:T(8,128)} %bitcast.21, f32[1024,256]{1,0:T(8,128)} %bitcast.22, f32[1024,256]{1,0:T(8,128)} %bitcast.23, s32[16,128]{1,0:T(8,128)} %bitcast.28, s32[16,128]{1,0:T(8,128)} %bitcast.29, ...), custom_call_target="tpu_custom_call" | custom-call | flops 30000001024 | bytes 4194304 | tf_op jit(solution)/shard_map/viscous_steps/pallas_call | solution.py:583
  98.0 42.6 %surrogate.1 = (f32[128,8,128]{2,1,0:T(8,128)}, f32[1024,256]{1,0:T(8,128)}) custom-call(s32[8192]{0:T(1024)} %bitcast.17, f32[8,256]{1,0:T(8,128)} %get-tuple-element.20.feats, f32[8,256]{1,0:T(8,128)} %get-tuple-element.21.target, f32[1,128]{1,0:T(1,128)} %bitcast.18, f32[1,128]{1,0:T(1,128)} %bitcast.19, f32[2,128]{1,0:T(2,128)} %bias_ref.1, ...), custom_call_target="tpu_custom_call" | custom-call | tf_op jit(solution)/shard_map/surrogate/pallas_call | solution.py:882
  140.6 22.6 %sum_grads.1.tiles = f32[128,8,128]{2,1,0:T(8,128)} custom-call(f32[128,8,128]{2,1,0:T(8,128)} %get-tuple-element.24.grads_hbm), custom_call_target="tpu_custom_call" | custom-call | tf_op jit(solution)/shard_map/sum_grads/pallas_call | solution.py:969
  163.2 1.8 %unpack.1 = (f32[2,256,128]{2,1,0:T(8,128)}, f32[1,128]{1,0:T(1,128)}, f32[1,128]{1,0:T(1,128)}, f32[2,128]{1,0:T(2,128)}, f32[1,128]{1,0:T(1,128)}, /*index=5*/f32[1,1]{1,0:T(1,128)}) custom-call(f32[128,8,128]{2,1,0:T(8,128)} %sum_grads.1.tiles), custom_call_target="tpu_custom_call" | custom-call | tf_op jit(solution)/shard_map/unpack/pallas_call | solution.py:1001

commit v4 on v3

--- a/solution.py
+++ b/solution.py
@@ -351,21 +351,18 @@
         buffer[call, mine] = jnp.broadcast_to(message, (8, 128))
         own = buffer.at[call, mine]
         for o in range(1, n):
-            remote(own, own, send.at[call, o], recv.at[call, mine], peer(o)[1]).start()
+            remote(own, own, send.at[call], recv.at[call], peer(o)[1]).start()
 
     def reduce_wait(call, which):
         buffer, send, recv, peer, mine, n = stages[which]
-        own = buffer.at[call, mine]
-        for o in range(1, n):
-            other, who = peer(o)
-            slot = buffer.at[call, other]
-            remote(slot, slot, send.at[call, o], recv.at[call, other], who).wait_recv()
-        for o in range(1, n):
-            remote(own, own, send.at[call, o], recv.at[call, mine], peer(o)[1]).wait_send()
-        total = buffer[call, 0]
-        for i in range(1, n):
-            total = total + buffer[call, i]
-        return total
+        arrived = buffer.at[call, pl.ds(0, n - 1)]
+        copy = remote(arrived, arrived, send.at[call], recv.at[call], peer(1)[1])
+        copy.wait_recv()
+        copy.wait_send()
+        parts = [buffer[call, i] for i in range(n)]
+        while len(parts) > 1:
+            parts = [a + b for a, b in zip(parts[::2], parts[1::2])]
+        return parts[0]
 
     def reduce_start(call, count):
         total = jnp.sum(dots[...], axis=1)
@@ -459,6 +456,7 @@
             picked = []
             pick(out[...], sample, hot_sample, lambda i, row: picked.append(row))
             table[step - 1, pl.ds(pl.multiple_of(me * 8, 8), 8), :] = jnp.concatenate(picked, axis=0)
+            start_all(peer_copies(step - 1))
             exchange_wait(2 * step, 0, True)
         follow(1)
         index = {}
@@ -473,8 +471,6 @@
         reduce_middle(call)
         if step == 0:
             onehot_rows(part, hot_part)
-        else:
-            start_all(peer_copies(step - 1))
         exchange_wait(2 * step + 1, 3, False)
         follow(4)
         m = reduce_end(call, 9)
@@ -608,8 +604,8 @@
             pltpu.VMEM((ROWS, NODES), BF16),
             dma((4, 2)), dma((4, 2)),
             dma((2, 2)), dma((2, 2)),
-            dma((4, 8)), dma((4, 8)),
-            dma((4, 16)), dma((4, 16)),
+            dma((4,)), dma((4,)),
+            dma((4,)), dma((4,)),
             dma((2,)), dma((2,)),
             dma((2,)), dma((2,)),
         ],

time: 168 us -> 163 us (0.970)
  Pallas kernels: 164 us -> 159 us
    pallas_call x1, Pallas kernels: 97.4 us -> 92 us  [run_steps(): pl.pallas_call(steps_kernel, out_shape=(jax.ShapeDtypeStruct((ROWS, 256),...]
where the time goes in v4:
time: 163 us; the launch traced here: 160 us
  Pallas kernels  159 us (98%)
    pallas_call x1, Pallas kernels, run_steps(): pl.pallas_call(steps_kernel, out_shape=(jax.ShapeDtypeStruct((ROWS, 256),...  92 us
    pallas_call x1, Pallas kernels, surrogate(): pl.pallas_call(surrogate_kernel, out_shape=(jax.ShapeDtypeStruct((128, 8,...  42.6 us
    pallas_call x1, Pallas kernels, sum_grads(): pl.pallas_call(sum_kernel, out_shape=jax.ShapeDtypeStruct((128, 8, 128),...  22.8 us

profile of v4, /device:TPU:1, one launch (start us, length us, event | category | flops | bytes accessed | tf_op | source)
XLA Modules:
  0.0 160.2 jit_solution(13964843636197052897)
XLA Ops:
  0.6 92.0 %viscous_steps.1 = (f32[1024,256]{1,0:T(8,128)}, f32[8,256]{1,0:T(8,128)}, f32[8,256]{1,0:T(8,128)}, s32[64,128]{1,0:T(8,128)}) custom-call(f32[1024,256]{1,0:T(8,128)} %bitcast.21, f32[1024,256]{1,0:T(8,128)} %bitcast.22, f32[1024,256]{1,0:T(8,128)} %bitcast.23, s32[16,128]{1,0:T(8,128)} %bitcast.28, s32[16,128]{1,0:T(8,128)} %bitcast.29, ...), custom_call_target="tpu_custom_call" | custom-call | flops 30000001024 | bytes 4194304 | tf_op jit(solution)/shard_map/viscous_steps/pallas_call | solution.py:579
  92.7 42.6 %surrogate.1 = (f32[128,8,128]{2,1,0:T(8,128)}, f32[1024,256]{1,0:T(8,128)}) custom-call(s32[8192]{0:T(1024)} %bitcast.17, f32[8,256]{1,0:T(8,128)} %get-tuple-element.20.feats, f32[8,256]{1,0:T(8,128)} %get-tuple-element.21.target, f32[1,128]{1,0:T(1,128)} %bitcast.18, f32[1,128]{1,0:T(1,128)} %bitcast.19, f32[2,128]{1,0:T(2,128)} %bias_ref.1, ...), custom_call_target="tpu_custom_call" | custom-call | tf_op jit(solution)/shard_map/surrogate/pallas_call | solution.py:878
  135.3 22.8 %sum_grads.1.tiles = f32[128,8,128]{2,1,0:T(8,128)} custom-call(f32[128,8,128]{2,1,0:T(8,128)} %get-tuple-element.24.grads_hbm), custom_call_target="tpu_custom_call" | custom-call | tf_op jit(solution)/shard_map/sum_grads/pallas_call | solution.py:965
  158.1 1.8 %unpack.1 = (f32[2,256,128]{2,1,0:T(8,128)}, f32[1,128]{1,0:T(1,128)}, f32[1,128]{1,0:T(1,128)}, f32[2,128]{1,0:T(2,128)}, f32[1,128]{1,0:T(1,128)}, /*index=5*/f32[1,1]{1,0:T(1,128)}) custom-call(f32[128,8,128]{2,1,0:T(8,128)} %sum_grads.1.tiles), custom_call_target="tpu_custom_call" | custom-call | tf_op jit(solution)/shard_map/unpack/pallas_call | solution.py:997
